TPU v7x, 32 devices: a whole 2x2x4 slice. The times are simulated.
32 devices in a mesh: gx: 4 (over z), gy: 2 (over x), gz: 4 (over y, core).
Axes of the slice: x: 2, y: 2, z: 4, core: 2. Of those that a mesh axis runs over, the one named last changes fastest.
Arguments:
- populations: float32 [19, 8, 16, 512], P(None, ('gy', 'gz'), 'gx'), may hold values from 0.5 to 1.5
- viscosity: float32 [8, 16, 512], P(('gy', 'gz'), 'gx'), may hold values from 0.01 to 0.3
- links: int32 [8, 16, 512], P(('gy', 'gz'), 'gx'), may hold values from 0 to 262143, as said below
- flags: int32 [8, 16, 512], P(('gy', 'gz'), 'gx'), may hold values from 0 to 2, as said below
- neighbours: int32 [8, 16, 18], P(('gy', 'gz'), 'gx'), may hold values from -1 to 15, as said below
- owners: int32 [8, 16], P(('gy', 'gz')), may hold values from 0 to 3, as said below
- slots: int32 [8, 16], P(('gy', 'gz')), may hold values from 0 to 15, as said below
- concentrations: float32 [4, 32, 16, 512], P(None, 'gx', 'gy', 'gz'), may hold values from 0.2 to 2
- diffusivity: float32 [32, 16, 512], P('gx', 'gy', 'gz'), may hold values from 0.04 to 0.12
- uptake_rate: float32 [32, 16, 512], P('gx', 'gy', 'gz'), may hold values from 0.02 to 0.2
Outputs:
- weighted_populations: float32 [19, 8, 16, 512], P(None, ('gy', 'gz'), 'gx')
- tissue_conc: float32 [4, 32, 16, 512], P(None, 'gx', 'gy', 'gz')
Inputs may be any that keep to these rules, and one draw needn't show every extreme that they name: `links`: bit i - 1 is set when the link of population i into the site is open. `flags`: 0 interior site, 1 inlet site, 2 outlet site. `neighbours`: -1 where no block lies beside; the relation is mutual: if block b has N in direction k, N has b in the opposite direction; a block beside lies in the list of the same index of gx or of the one next to it. `owners`: no two of the 4 blocks on one index of gx have the same owner, and in every segment some owner receives exactly 1 from every index of gx. `slots`: distinct among the blocks of one segment with one owner.
All inputs are finite; a program needn't handle non-finite values.
Results may differ from a plain program's by a relative error of at most 0.0003.
Values sent between devices are 32-bit elements; how exact they have to be, the bound alone decides.
A program may use at most 128 MiB of HBM per device.

v0:
```python
import jax
import jax.numpy as jnp
import numpy as np
from jax import lax
from jax.sharding import PartitionSpec as P

FLOW_STEPS = 4
TISSUE_STEPS = 3


LATTICE_DIRS = (
    (0, 0, 0),
    (1, 0, 0),
    (-1, 0, 0),
    (0, 1, 0),
    (0, -1, 0),
    (0, 0, 1),
    (0, 0, -1),
    (1, 1, 0),
    (-1, -1, 0),
    (1, -1, 0),
    (-1, 1, 0),
    (1, 0, 1),
    (-1, 0, -1),
    (1, 0, -1),
    (-1, 0, 1),
    (0, 1, 1),
    (0, -1, -1),
    (0, 1, -1),
    (0, -1, 1),
)
DIFFUSION_GAIN = (1.0, 0.6, 0.7, 0.35)
HALF_SATURATION = (0.3, 0.5, 0.8, 0.2)
ADVECT_GAIN = 3.0
INLET_DENSITY = 1.03
OUTLET_DENSITY = 0.97


def padded(cells, sides, width):
    for axis, dim in sides:
        count = lax.axis_size(axis)
        ends = count - 1
        head = lax.slice_in_dim(cells, 0, width, axis=dim)
        tail = lax.slice_in_dim(cells, cells.shape[dim] - width, cells.shape[dim], axis=dim)
        cells = jnp.concatenate(
            [
                lax.ppermute(tail, axis, [(i, (i + 1) % count) for i in range(ends)]),
                cells,
                lax.ppermute(head, axis, [((i + 1) % count, i) for i in range(ends)]),
            ],
            axis=dim,
        )
    return cells


def lattice_tables():
    vectors = np.array(LATTICE_DIRS, dtype=np.int64)
    weights = np.array([1.0 / 3.0] + [1.0 / 18.0] * 6 + [1.0 / 36.0] * 12)
    opposite = [
        LATTICE_DIRS.index(tuple((-part_val for part_val in LATTICE_DIRS[member])))
        for member in range(19)
    ]
    sites = np.arange(512)
    coords = np.stack([sites // 64, sites // 8 % 8, sites % 8], axis=1)
    stride = np.array([64, 8, 1])
    position = {}
    rim_source = []
    for member in range(1, 19):
        moved = coords + vectors[member]
        leaving = ((moved < 0) | (moved > 7)).any(axis=1)
        chosen = sites[leaving]
        for site_id in chosen:
            position[member, int(site_id)] = len(rim_source)
            rim_source.append(member * 512 + int(site_id))
    rim_width = -(-len(rim_source) // 128) * 128
    request_dir = []
    request_pos = []
    offsets = [0]
    counts = [0]
    selects = [sites.copy()]
    dir_maps = [np.zeros(512, np.int64)]
    arriving_masks = [np.zeros(512, bool)]
    shifts = [0]
    for member in range(1, 19):
        source = coords - vectors[member]
        arriving = ((source < 0) | (source > 7)).any(axis=1)
        select = sites.copy()
        dir_map = np.zeros(512, np.int64)
        offsets.append(len(request_dir))
        counts.append(int(arriving.sum()))
        for rank_pos, site_id in enumerate(sites[arriving]):
            block_dir = tuple((int(part_val) for part_val in source[site_id] // 8))
            dir_index = LATTICE_DIRS.index(block_dir) - 1
            local_site = int((source[site_id] % 8 * stride).sum())
            request_dir.append(dir_index)
            request_pos.append(position[member, local_site])
            select[site_id] = 512 + rank_pos
            dir_map[site_id] = dir_index
        selects.append(select)
        dir_maps.append(dir_map)
        arriving_masks.append(arriving)
        shifts.append(int((vectors[member] * stride).sum()))
    request_width = -(-len(request_dir) // 128) * 128
    request_dir = request_dir + [0] * (request_width - len(request_dir))
    request_pos = request_pos + [0] * (request_width - len(request_pos))
    return {
        "vectors": vectors,
        "weights": weights,
        "opposite": opposite,
        "rim_source": np.array(rim_source),
        "rim_width": rim_width,
        "request_dir": np.array(request_dir),
        "request_pos": np.array(request_pos),
        "offsets": offsets,
        "counts": counts,
        "selects": selects,
        "dir_maps": dir_maps,
        "arriving": arriving_masks,
        "shifts": shifts,
    }


def equilibrium(density, momentum, vectors, weights):
    project = jnp.tensordot(vectors, momentum, axes=1, precision=lax.Precision.HIGHEST)
    square = jnp.sum(momentum * momentum, axis=0)
    return weights[:, None, None] * (
        density + 3.0 * project + 4.5 * project * project - 1.5 * square
    )


def collide(popul, relax, vectors, weights):
    density = jnp.sum(popul, axis=0)
    momentum = jnp.tensordot(vectors.T, popul, axes=1, precision=lax.Precision.HIGHEST)
    return popul - relax * (popul - equilibrium(density, momentum, vectors, weights))


def rim_rows(post, tables):
    block_count = post.shape[1]
    flat = jnp.transpose(post, (1, 0, 2)).reshape(block_count, 19 * 512)
    rim = jnp.take(flat, jnp.asarray(tables["rim_source"], jnp.int32), axis=1)
    return jnp.pad(rim, ((0, 0), (0, tables["rim_width"] - rim.shape[1])))


def stream(post, arrived, link_bits, beside_ids, tables):
    result = [post[0]]
    for member in range(1, 19):
        rolled = jnp.roll(post[member], tables["shifts"][member], axis=-1)
        start_col = tables["offsets"][member]
        pool = jnp.concatenate(
            [rolled, arrived[:, start_col : start_col + tables["counts"][member]]], axis=1
        )
        pulled = jnp.take(pool, jnp.asarray(tables["selects"][member], jnp.int32), axis=1)
        beside = (
            jnp.take(beside_ids, jnp.asarray(tables["dir_maps"][member], jnp.int32), axis=1) >= 0
        )
        link_open = jnp.right_shift(link_bits, member - 1) % 2 == 1
        arriving = jnp.asarray(tables["arriving"][member])[None, :]
        opened = link_open & (beside | jnp.logical_not(arriving))
        result.append(jnp.where(opened, pulled, post[tables["opposite"][member]]))
    return jnp.stack(result)


def boundary(popul, site_flags, vectors, weights):
    momentum = jnp.tensordot(vectors.T, popul, axes=1, precision=lax.Precision.HIGHEST)
    density = jnp.where(site_flags == 1, INLET_DENSITY, OUTLET_DENSITY)
    settled = equilibrium(density, momentum, vectors, weights)
    return jnp.where(site_flags[None] > 0, settled, popul)


def shifted(field, offset):
    extent_x, extent_y, extent_z = field.shape[-3:]
    step_x, step_y, step_z = offset
    return field[
        ...,
        1 + step_x : extent_x - 1 + step_x,
        1 + step_y : extent_y - 1 + step_y,
        1 + step_z : extent_z - 1 + step_z,
    ]


def tissue_step(conc_ext, diff_ext, uptake_here, velocity):
    center = conc_ext[:, 1:-1, 1:-1, 1:-1]
    diff_mid = diff_ext[1:-1, 1:-1, 1:-1]
    spread = jnp.zeros_like(center)
    for offset in ((1, 0, 0), (-1, 0, 0), (0, 1, 0), (0, -1, 0), (0, 0, 1), (0, 0, -1)):
        beside_conc = shifted(conc_ext, offset)
        beside_diff = shifted(diff_ext, offset)
        spread = spread + 0.5 * (diff_mid + beside_diff) * (beside_conc - center)
    drifted = jnp.zeros_like(center)
    for axis_pos in range(3):
        unit_vec = [0, 0, 0]
        unit_vec[axis_pos] = 1
        ahead = shifted(conc_ext, tuple(unit_vec))
        behind = shifted(conc_ext, tuple((-part_val for part_val in unit_vec)))
        speed_axis = ADVECT_GAIN * velocity[axis_pos]
        drifted = (
            drifted
            - jnp.maximum(speed_axis, 0.0) * (center - behind)
            - jnp.minimum(speed_axis, 0.0) * (ahead - center)
        )
    species_gain = jnp.array(DIFFUSION_GAIN, jnp.float32)[:, None, None, None]
    halfsat = jnp.array(HALF_SATURATION, jnp.float32)[:, None, None, None]
    uptake = uptake_here * center / (halfsat + jnp.abs(center))
    reaction = jnp.stack([-uptake[0], -uptake[1], 2.0 * uptake[1], -uptake[3]])
    return center + species_gain * spread + drifted + reaction


def shards(
    populations,
    viscosity,
    links,
    flags,
    neighbours,
    owners,
    slots,
    concentrations,
    diffusivity,
    uptake_rate,
):
    tables = lattice_tables()
    weights = jnp.asarray(tables["weights"], jnp.float32)
    vectors = jnp.asarray(tables["vectors"], jnp.float32)
    popul = populations[:, 0] * weights[:, None, None]
    relax = 1.0 / (3.0 * viscosity[0] + 0.5)
    link_bits = links[0]
    site_flags = flags[0]
    beside_ids = neighbours[0]
    block_count = popul.shape[1]
    request_block = jnp.take(beside_ids, jnp.asarray(tables["request_dir"], jnp.int32), axis=1)
    request_pos = jnp.asarray(tables["request_pos"], jnp.int32)
    first_block = (lax.axis_index("gx") - 1) * block_count
    local_block = request_block - first_block
    valid = (local_block >= 0) & (local_block < 3 * block_count)
    for turn_index in range(FLOW_STEPS):
        post = collide(popul, relax, vectors, weights)
        rim = rim_rows(post, tables)
        extended = padded(rim, (("gx", 0),), block_count)
        flat_index = (
            jnp.clip(local_block, 0, 3 * block_count - 1) * extended.shape[1] + request_pos[None, :]
        )
        arrived = jnp.where(valid, jnp.take(extended.reshape(-1), flat_index), 0.0)
        popul = stream(post, arrived, link_bits, beside_ids, tables)
        popul = boundary(popul, site_flags, vectors, weights)
    weighted = (popul / weights[:, None, None])[:, None]
    momentum = jnp.tensordot(vectors.T, popul, axes=1, precision=lax.Precision.HIGHEST)
    block_rows = jnp.transpose(momentum, (1, 0, 2)).reshape(block_count, 3 * 512)
    extent_x, extent_y, extent_z = concentrations.shape[1:]
    slot_x = extent_x // 8
    slot_y = extent_y // 8
    slot_z = extent_z // 8
    slot_total = slot_x * slot_y * slot_z
    owner_all = owners[0]
    slot_all = slots[0]
    my_index = lax.axis_index("gx")
    slot_ids = jnp.arange(slot_total, dtype=jnp.int32)
    start_blocks = jnp.zeros((slot_total, 3 * 512), jnp.float32)
    piece = jax.tree.map(lambda part: lax.all_gather(part, "gx", axis=0, tiled=True), block_rows)
    row_count = piece.shape[0]
    piece_owner = lax.slice_in_dim(owner_all, 0, row_count, axis=0)
    piece_slot = lax.slice_in_dim(slot_all, 0, row_count, axis=0)
    hit = (piece_owner[None, :] == my_index) & (piece_slot[None, :] == slot_ids[:, None])
    brick_blocks = start_blocks + jnp.dot(
        hit.astype(jnp.float32), piece, precision=lax.Precision.HIGHEST
    )
    velocity = (
        brick_blocks.reshape(slot_x, slot_y, slot_z, 3, 8, 8, 8)
        .transpose(3, 0, 4, 1, 5, 2, 6)
        .reshape(3, extent_x, extent_y, extent_z)
    )
    conc_ext, diff_ext = (
        padded(concentrations, (("gx", 1), ("gy", 2), ("gz", 3)), 1),
        padded(diffusivity[None], (("gx", 1), ("gy", 2), ("gz", 3)), 1),
    )
    diff_ext = diff_ext[0]
    conc = tissue_step(conc_ext, diff_ext, uptake_rate, velocity)
    for turn_index in range(TISSUE_STEPS - 1):
        conc_ext = padded(conc, (("gx", 1), ("gy", 2), ("gz", 3)), 1)
        conc = tissue_step(conc_ext, diff_ext, uptake_rate, velocity)
    return (weighted, conc)


def solution(mesh):
    return jax.shard_map(
        shards,
        mesh=mesh,
        in_specs=(
            P(None, ("gy", "gz"), "gx", None),
            P(("gy", "gz"), "gx", None),
            P(("gy", "gz"), "gx", None),
            P(("gy", "gz"), "gx", None),
            P(("gy", "gz"), "gx", None),
            P(("gy", "gz"), None),
            P(("gy", "gz"), None),
            P(None, "gx", "gy", "gz"),
            P("gx", "gy", "gz"),
            P("gx", "gy", "gz"),
        ),
        out_specs=(P(None, ("gy", "gz"), "gx", None), P(None, "gx", "gy", "gz")),
        check_vma=False,
    )
```

profile of v0, /device:TPU:22, one launch (start us, length us, event | category | flops | bytes accessed | tf_op | source)
XLA Modules:
  0.0 488.0 jit_solution(10525933543536940901)
XLA Ops:
  0.7 1.1 fusion.244
  2.8 1.1 fusion.263
  6.0 3.0 copy.945
  9.0 5.8 %gather_fusion.2 = f32[1824,4]{1,0:T(8,128)S(1)} fusion(f32[4,9728]{0,1:T(8,128)} %bitcast.1073, s32[2048]{0:T(1024)S(1)} %get-tuple-element.326), kind=kCustom, calls=%fused_computation.1.clone | custom fusion | bytes 65664 | tf_op jit(solution)/shard_map/jit(_take)/gather | solution.py:140
  15.1 3.5 collective-permute-start
  18.6 2.4 collective-permute-start.1
  21.0 3.5 collective-permute-start.8
  24.5 2.4 collective-permute-start.9
  26.9 3.5 collective-permute-start.15
  30.7 3.5 gather_fusion
  34.6 1.2 compare_bitcast_fusion.1
  38.4 1.3 collective-permute-start.10
  39.7 4.5 collective-permute-start.11
  46.7 1.0 gather_fusion.7
  49.1 1.0 gather_fusion.11
  50.3 1.0 gather_fusion.13
  52.7 1.0 gather_fusion.17
  63.6 1.9 collective-permute-start.12
  65.5 3.6 collective-permute-start.13
  71.5 2.4 collective-permute-start.14
  74.3 2.8 collective-permute-done.14
  77.1 1.3 collective-permute-start.16
  78.4 1.8 collective-permute-start.17
  80.4 39.8 %gather_fusion.3 = f32[7680]{0:T(1024)S(1)} fusion(f32[23040]{0:T(1024)S(1)} %reshape.235, s32[8192]{0:T(1024)S(1)} %pad_clamp_fusion), kind=kCustom, calls=%fused_computation.2.clone | custom fusion | bytes 92160 | tf_op jit(solution)/shard_map/jit(_take)/gather | solution.py:241
  149.1 3.0 copy.795
  152.1 5.8 %gather_fusion.39 = f32[1824,4]{1,0:T(8,128)S(1)} fusion(f32[4,9728]{0,1:T(8,128)} %copy.795, s32[2048]{0:T(1024)S(1)} %get-tuple-element.326), kind=kCustom, calls=%fused_computation.22.clone | custom fusion | bytes 65664 | tf_op jit(solution)/shard_map/jit(_take)/gather | solution.py:140
  158.3 1.9 collective-permute-start.2
  160.2 3.9 collective-permute-start.3
  165.3 1.9 collective-permute-start.18
  167.2 2.6 collective-permute-start.19
  169.9 39.8 %gather_fusion.40 = f32[7680]{0:T(1024)S(1)} fusion(f32[23040]{0:T(1024)S(1)} %reshape.237, s32[8192]{0:T(1024)S(1)} %pad_clamp_fusion), kind=kCustom, calls=%fused_computation.25.clone | custom fusion | bytes 92160 | tf_op jit(solution)/shard_map/jit(_take)/gather | solution.py:241
  238.7 3.0 copy.843
  241.7 5.8 %gather_fusion.59 = f32[1824,4]{1,0:T(8,128)S(1)} fusion(f32[4,9728]{0,1:T(8,128)} %copy.843, s32[2048]{0:T(1024)S(1)} %get-tuple-element.326), kind=kCustom, calls=%fused_computation.23.clone | custom fusion | bytes 65664 | tf_op jit(solution)/shard_map/jit(_take)/gather | solution.py:140
  247.9 1.9 collective-permute-start.4
  249.8 4.1 collective-permute-start.5
  254.1 1.6 collective-permute-done.5
  255.7 39.8 %gather_fusion.60 = f32[7680]{0:T(1024)S(1)} fusion(f32[23040]{0:T(1024)S(1)} %reshape.239, s32[8192]{0:T(1024)S(1)} %pad_clamp_fusion), kind=kCustom, calls=%fused_computation.26.clone | custom fusion | bytes 92160 | tf_op jit(solution)/shard_map/jit(_take)/gather | solution.py:241
  324.5 3.0 copy.891
  327.5 5.8 %gather_fusion.79 = f32[1824,4]{1,0:T(8,128)S(1)} fusion(f32[4,9728]{0,1:T(8,128)} %copy.891, s32[2048]{0:T(1024)S(1)} %get-tuple-element.326), kind=kCustom, calls=%fused_computation.24.clone | custom fusion | bytes 65664 | tf_op jit(solution)/shard_map/jit(_take)/gather | solution.py:140
  333.7 1.9 collective-permute-start.6
  335.6 4.2 collective-permute-start.7
  339.9 1.5 collective-permute-done.7
  341.4 39.8 %gather_fusion.80 = f32[7680]{0:T(1024)S(1)} fusion(f32[23040]{0:T(1024)S(1)} %reshape.241, s32[8192]{0:T(1024)S(1)} %pad_clamp_fusion), kind=kCustom, calls=%fused_computation.27.clone | custom fusion | bytes 92160 | tf_op jit(solution)/shard_map/jit(_take)/gather | solution.py:241
  410.4 14.7 %all-gather = f32[4,4,1536]{2,1,0:T(4,128)S(1)} all-gather(f32[1,4,1536]{2,1,0:T(4,128)S(1)} %reshape.1045), channel_id=1, replica_groups=mesh['gx'=4,'gy'=2,'gz'=4] {'gx'}, dimensions={0}, use_global_device_ids=true | all-gather | bytes 122880 | tf_op jit(solution)/shard_map/all_gather | solution.py:257
  429.5 1.9 collective-permute-start.20
  431.4 3.9 collective-permute-start.21
  435.3 2.6 collective-permute-done.21
  437.9 4.5 collective-permute-start.22
  442.5 1.3 collective-permute-start.23
  443.9 4.2 collective-permute-done.23
  448.4 1.9 collective-permute-start.24
  450.3 2.4 collective-permute-start.25
  452.8 2.1 collective-permute-done.24
  454.9 3.8 collective-permute-done.25
  459.1 3.9 collective-permute-start.26
  463.0 1.9 collective-permute-start.27
  464.9 3.7 collective-permute-done.27
  468.7 1.6 collective-permute-start.28
  470.3 1.3 collective-permute-start.29
  471.8 4.2 collective-permute-done.29
  476.2 1.9 collective-permute-start.30
  478.1 2.4 collective-permute-start.31
  480.6 2.1 collective-permute-done.30
  482.7 3.8 collective-permute-done.31
  (799 shorter events, 146.9 us)
Async XLA Ops:
  4.6 33.3 %copy-start.42 = (s32[512]{0:T(512)S(1)}, s32[512]{0:T(512)}, u32[]{:S(2)}) copy-start(s32[512]{0:T(512)} %constant.1468) | copy-start | bytes 6148
  4.6 33.2 %copy-start.40 = (s32[512]{0:T(512)S(1)}, s32[512]{0:T(512)}, u32[]{:S(2)}) copy-start(s32[512]{0:T(512)} %constant.1470) | copy-start | bytes 6148
  4.7 33.3 %copy-start.38 = (s32[512]{0:T(512)S(1)}, s32[512]{0:T(512)}, u32[]{:S(2)}) copy-start(s32[512]{0:T(512)} %constant.1472) | copy-start | bytes 6148
  4.7 33.3 %copy-start.39 = (s32[512]{0:T(512)S(1)}, s32[512]{0:T(512)}, u32[]{:S(2)}) copy-start(s32[512]{0:T(512)} %constant.1473) | copy-start | bytes 6148
  4.7 33.3 %copy-start.36 = (s32[512]{0:T(512)S(1)}, s32[512]{0:T(512)}, u32[]{:S(2)}) copy-start(s32[512]{0:T(512)} %constant.1474) | copy-start | bytes 6148
  4.7 33.3 %copy-start.37 = (s32[512]{0:T(512)S(1)}, s32[512]{0:T(512)}, u32[]{:S(2)}) copy-start(s32[512]{0:T(512)} %constant.1475) | copy-start | bytes 6148
  4.7 33.3 %copy-start.34 = (s32[512]{0:T(512)S(1)}, s32[512]{0:T(512)}, u32[]{:S(2)}) copy-start(s32[512]{0:T(512)} %constant.1476) | copy-start | bytes 6148
  4.7 33.3 %copy-start.35 = (s32[512]{0:T(512)S(1)}, s32[512]{0:T(512)}, u32[]{:S(2)}) copy-start(s32[512]{0:T(512)} %constant.1477) | copy-start | bytes 6148
  4.7 33.3 %copy-start.32 = (s32[512]{0:T(512)S(1)}, s32[512]{0:T(512)}, u32[]{:S(2)}) copy-start(s32[512]{0:T(512)} %constant.1478) | copy-start | bytes 6148
  4.7 33.3 %copy-start.33 = (s32[512]{0:T(512)S(1)}, s32[512]{0:T(512)}, u32[]{:S(2)}) copy-start(s32[512]{0:T(512)} %constant.1479) | copy-start | bytes 6148
  4.8 33.3 %copy-start.30 = (s32[512]{0:T(512)S(1)}, s32[512]{0:T(512)}, u32[]{:S(2)}) copy-start(s32[512]{0:T(512)} %constant.1480) | copy-start | bytes 6148
  4.8 33.3 %copy-start.31 = (s32[512]{0:T(512)S(1)}, s32[512]{0:T(512)}, u32[]{:S(2)}) copy-start(s32[512]{0:T(512)} %constant.1481) | copy-start | bytes 6148
  4.8 33.3 %copy-start.28 = (s32[512]{0:T(512)S(1)}, s32[512]{0:T(512)}, u32[]{:S(2)}) copy-start(s32[512]{0:T(512)} %constant.1482) | copy-start | bytes 6148
  4.8 33.3 %copy-start.29 = (s32[512]{0:T(512)S(1)}, s32[512]{0:T(512)}, u32[]{:S(2)}) copy-start(s32[512]{0:T(512)} %constant.1483) | copy-start | bytes 6148
  4.8 33.3 %copy-start.26 = (s32[512]{0:T(512)S(1)}, s32[512]{0:T(512)}, u32[]{:S(2)}) copy-start(s32[512]{0:T(512)} %constant.1484) | copy-start | bytes 6148
  4.8 33.3 %copy-start.27 = (s32[512]{0:T(512)S(1)}, s32[512]{0:T(512)}, u32[]{:S(2)}) copy-start(s32[512]{0:T(512)} %constant.1485) | copy-start | bytes 6148
  4.8 33.3 %copy-start.24 = (s32[512]{0:T(512)S(1)}, s32[512]{0:T(512)}, u32[]{:S(2)}) copy-start(s32[512]{0:T(512)} %constant.1486) | copy-start | bytes 6148
  4.8 33.3 %copy-start.25 = (s32[512]{0:T(512)S(1)}, s32[512]{0:T(512)}, u32[]{:S(2)}) copy-start(s32[512]{0:T(512)} %constant.1487) | copy-start | bytes 6148
  4.9 33.4 %copy-start.22 = (s32[512]{0:T(512)S(1)}, s32[512]{0:T(512)}, u32[]{:S(2)}) copy-start(s32[512]{0:T(512)} %constant.1488) | copy-start | bytes 6148
  4.9 33.4 %copy-start.23 = (s32[512]{0:T(512)S(1)}, s32[512]{0:T(512)}, u32[]{:S(2)}) copy-start(s32[512]{0:T(512)} %constant.1489) | copy-start | bytes 6148
  5.1 33.3 %copy-start.16 = (s32[512]{0:T(512)S(1)}, s32[512]{0:T(512)}, u32[]{:S(2)}) copy-start(s32[512]{0:T(512)} %constant.1494) | copy-start | bytes 6148
  5.1 33.3 %copy-start.17 = (s32[512]{0:T(512)S(1)}, s32[512]{0:T(512)}, u32[]{:S(2)}) copy-start(s32[512]{0:T(512)} %constant.1495) | copy-start | bytes 6148
  5.1 39.2 %copy-start.14 = (s32[512]{0:T(512)S(1)}, s32[512]{0:T(512)}, u32[]{:S(2)}) copy-start(s32[512]{0:T(512)} %constant.1496) | copy-start | bytes 6148
  5.1 39.2 %copy-start.15 = (s32[512]{0:T(512)S(1)}, s32[512]{0:T(512)}, u32[]{:S(2)}) copy-start(s32[512]{0:T(512)} %constant.1497) | copy-start | bytes 6148
  15.1 65.1 %collective-permute-start = (f32[4,1920]{1,0:T(4,128)S(1)}, f32[4,1920]{1,0:T(4,128)S(1)}, u32[]{:S(2)}, u32[]{:S(2)}) collective-permute-start(f32[4,1920]{1,0:T(4,128)S(1)} %pad.13.clone), channel_id=1, source_target_pairs={{0,8},{8,16},{16,24},{1,9},{9,17},{17,25},{2,10},{10,18},{18,26},{... | collective-permute-start | bytes 92168 | tf_op jit(solution)/shard_map/ppermute | solution.py:47
  18.6 61.7 %collective-permute-start.1 = (f32[4,1920]{1,0:T(4,128)S(1)}, f32[4,1920]{1,0:T(4,128)S(1)}, u32[]{:S(2)}, u32[]{:S(2)}) collective-permute-start(f32[4,1920]{1,0:T(4,128)S(1)} %pad.13.clone), channel_id=1, source_target_pairs={{8,0},{16,8},{24,16},{9,1},{17,9},{25,17},{10,2},{18,10},{26,18},{... | collective-permute-start | bytes 92168 | tf_op jit(solution)/shard_map/ppermute | solution.py:49
  21.0 17.3 %collective-permute-start.8 = (f32[1,1,8,128]{3,2,1,0:T(8,128)S(1)}, f32[1,1,8,128]{3,2,1,0:T(8,128)S(1)}, u32[]{:S(2)}, u32[]{:S(2)}) collective-permute-start(f32[1,1,8,128]{3,2,1,0:T(8,128)S(1)} %get-tuple-element.219), channel_id=1, source_target_pairs={{0,8},{8,16},{16,24},{1,9},{9,17},{17,25},{2,10},{10,18},{18,26},{... | collective-permute-start | bytes 12296 | tf_op jit(solution)/shard_map/ppermute | solution.py:47
  24.5 13.9 %collective-permute-start.9 = (f32[1,1,8,128]{3,2,1,0:T(8,128)S(1)}, f32[1,1,8,128]{3,2,1,0:T(8,128)S(1)}, u32[]{:S(2)}, u32[]{:S(2)}) collective-permute-start(f32[1,1,8,128]{3,2,1,0:T(8,128)S(1)} %get-tuple-element.220), channel_id=1, source_target_pairs={{8,0},{16,8},{24,16},{9,1},{17,9},{25,17},{10,2},{18,10},{26,18},{... | collective-permute-start | bytes 12296 | tf_op jit(solution)/shard_map/ppermute | solution.py:49
  26.9 47.3 %copy-start.4 = (f32[8,8,128]{2,1,0:T(8,128)S(1)}, f32[8,8,128]{2,1,0:T(8,128)}, u32[]{:S(2)}) copy-start(f32[8,8,128]{2,1,0:T(8,128)} %param.205) | copy-start | bytes 98308
  26.9 47.3 %copy-start.11 = (f32[4]{0:T(128)S(1)}, f32[4]{0:T(128)}, u32[]{:S(2)}) copy-start(f32[4]{0:T(128)} %constant.581.clone) | copy-start | bytes 52
  26.9 47.2 %collective-permute-start.15 = (f32[4,1,8,128]{3,2,1,0:T(8,128)S(1)}, f32[4,1,8,128]{3,2,1,0:T(8,128)S(1)}, u32[]{:S(2)}, u32[]{:S(2)}) collective-permute-start(f32[4,1,8,128]{3,2,1,0:T(8,128)S(1)} %get-tuple-element.208), channel_id=1, source_target_pairs={{0,8},{8,16},{16,24},{1,9},{9,17},{17,25},{2,10},{10,18},{18,26},{... | collective-permute-start | bytes 49160 | tf_op jit(solution)/shard_map/ppermute | solution.py:47
  38.4 25.1 %collective-permute-start.10 = (f32[1,10,1,128]{3,2,1,0:T(1,128)S(1)}, f32[1,10,1,128]{3,2,1,0:T(1,128)S(1)}, u32[]{:S(2)}, u32[]{:S(2)}) collective-permute-start(f32[1,10,1,128]{3,2,1,0:T(1,128)S(1)} %get-tuple-element.217), channel_id=1, source_target_pairs={{0,4},{1,5},{2,6},{3,7},{8,12},{9,13},{10,14},{11,15},{16,20},{17,... | collective-permute-start | bytes 15368 | tf_op jit(solution)/shard_map/ppermute | solution.py:47
  39.7 23.8 %collective-permute-start.11 = (f32[1,10,1,128]{3,2,1,0:T(1,128)S(1)}, f32[1,10,1,128]{3,2,1,0:T(1,128)S(1)}, u32[]{:S(2)}, u32[]{:S(2)}) collective-permute-start(f32[1,10,1,128]{3,2,1,0:T(1,128)S(1)} %get-tuple-element.218), channel_id=1, source_target_pairs={{4,0},{5,1},{6,2},{7,3},{12,8},{13,9},{14,10},{15,11},{20,16},{21,... | collective-permute-start | bytes 15368 | tf_op jit(solution)/shard_map/ppermute | solution.py:49
  63.6 7.9 %collective-permute-start.12 = (f32[1,10,10,1]{3,2,1,0:T(8,128)S(1)}, f32[1,10,10,1]{3,2,1,0:T(8,128)S(1)}, u32[]{:S(2)}, u32[]{:S(2)}) collective-permute-start(f32[1,10,10,1]{3,2,1,0:T(8,128)S(1)} %get-tuple-element.215), channel_id=1, source_target_pairs={{0,1},{1,2},{2,3},{4,5},{5,6},{6,7},{8,9},{9,10},{10,11},{12,13},{... | collective-permute-start | bytes 1208 | tf_op jit(solution)/shard_map/ppermute | solution.py:47
  65.5 8.3 %collective-permute-start.13 = (f32[1,10,10,1]{3,2,1,0:T(8,128)S(1)}, f32[1,10,10,1]{3,2,1,0:T(8,128)S(1)}, u32[]{:S(2)}, u32[]{:S(2)}) collective-permute-start(f32[1,10,10,1]{3,2,1,0:T(8,128)S(1)} %get-tuple-element.216), channel_id=1, source_target_pairs={{1,0},{2,1},{3,2},{5,4},{6,5},{7,6},{9,8},{10,9},{11,10},{13,12},{... | collective-permute-start | bytes 1208 | tf_op jit(solution)/shard_map/ppermute | solution.py:49
  71.5 5.6 %collective-permute-start.14 = (f32[4,1,8,128]{3,2,1,0:T(8,128)S(1)}, f32[4,1,8,128]{3,2,1,0:T(8,128)S(1)}, u32[]{:S(2)}, u32[]{:S(2)}) collective-permute-start(f32[4,1,8,128]{3,2,1,0:T(8,128)S(1)} %get-tuple-element.207), channel_id=1, source_target_pairs={{8,0},{16,8},{24,16},{9,1},{17,9},{25,17},{10,2},{18,10},{26,18},{... | collective-permute-start | bytes 49160 | tf_op jit(solution)/shard_map/ppermute | solution.py:49
  77.1 87.1 %collective-permute-start.16 = (f32[4,10,1,128]{3,2,1,0:T(1,128)S(1)}, f32[4,10,1,128]{3,2,1,0:T(1,128)S(1)}, u32[]{:S(2)}, u32[]{:S(2)}) collective-permute-start(f32[4,10,1,128]{3,2,1,0:T(1,128)S(1)} %get-tuple-element.110), channel_id=1, source_target_pairs={{4,0},{5,1},{6,2},{7,3},{12,8},{13,9},{14,10},{15,11},{20,16},{21,... | collective-permute-start | bytes 61448 | tf_op jit(solution)/shard_map/ppermute | solution.py:49
  78.4 85.8 %collective-permute-start.17 = (f32[4,10,1,128]{3,2,1,0:T(1,128)S(1)}, f32[4,10,1,128]{3,2,1,0:T(1,128)S(1)}, u32[]{:S(2)}, u32[]{:S(2)}) collective-permute-start(f32[4,10,1,128]{3,2,1,0:T(1,128)S(1)} %get-tuple-element.109), channel_id=1, source_target_pairs={{0,4},{1,5},{2,6},{3,7},{8,12},{9,13},{10,14},{11,15},{16,20},{17,... | collective-permute-start | bytes 61448 | tf_op jit(solution)/shard_map/ppermute | solution.py:47
  80.4 41.5 %copy-start = (s32[1,4,512]{2,1,0:T(4,128)S(1)}, s32[1,4,512]{2,1,0:T(4,128)}, u32[]{:S(2)}) copy-start(s32[1,4,512]{2,1,0:T(4,128)} %param.198) | copy-start | bytes 24580
  80.4 41.5 %copy-start.64 = (pred[512]{0:T(512)(128)(4,1)S(1)}, pred[512]{0:T(512)(128)(4,1)}, u32[]{:S(2)}) copy-start(pred[512]{0:T(512)(128)(4,1)} %constant.598) | copy-start | bytes 1540
  80.4 44.4 %copy-start.63 = (pred[512]{0:T(512)(128)(4,1)S(1)}, pred[512]{0:T(512)(128)(4,1)}, u32[]{:S(2)}) copy-start(pred[512]{0:T(512)(128)(4,1)} %constant.606) | copy-start | bytes 1540
  80.4 44.4 %copy-start.62 = (pred[512]{0:T(512)(128)(4,1)S(1)}, pred[512]{0:T(512)(128)(4,1)}, u32[]{:S(2)}) copy-start(pred[512]{0:T(512)(128)(4,1)} %constant.607) | copy-start | bytes 1540
  80.4 47.4 %copy-start.61 = (pred[512]{0:T(512)(128)(4,1)S(1)}, pred[512]{0:T(512)(128)(4,1)}, u32[]{:S(2)}) copy-start(pred[512]{0:T(512)(128)(4,1)} %constant.608) | copy-start | bytes 1540
  80.4 47.4 %copy-start.60 = (pred[512]{0:T(512)(128)(4,1)S(1)}, pred[512]{0:T(512)(128)(4,1)}, u32[]{:S(2)}) copy-start(pred[512]{0:T(512)(128)(4,1)} %constant.609) | copy-start | bytes 1540
  158.3 11.5 %collective-permute-start.2 = (f32[4,1920]{1,0:T(4,128)S(1)}, f32[4,1920]{1,0:T(4,128)S(1)}, u32[]{:S(2)}, u32[]{:S(2)}) collective-permute-start(f32[4,1920]{1,0:T(4,128)S(1)} %pad.14.clone), channel_id=1, source_target_pairs={{0,8},{8,16},{16,24},{1,9},{9,17},{17,25},{2,10},{10,18},{18,26},{... | collective-permute-start | bytes 92168 | tf_op jit(solution)/shard_map/ppermute | solution.py:47
  160.2 9.6 %collective-permute-start.3 = (f32[4,1920]{1,0:T(4,128)S(1)}, f32[4,1920]{1,0:T(4,128)S(1)}, u32[]{:S(2)}, u32[]{:S(2)}) collective-permute-start(f32[4,1920]{1,0:T(4,128)S(1)} %pad.14.clone), channel_id=1, source_target_pairs={{8,0},{16,8},{24,16},{9,1},{17,9},{25,17},{10,2},{18,10},{26,18},{... | collective-permute-start | bytes 92168 | tf_op jit(solution)/shard_map/ppermute | solution.py:49
  165.3 263.8 %collective-permute-start.18 = (f32[4,10,10,1]{3,2,1,0:T(8,128)}, f32[4,10,10,1]{3,2,1,0:T(8,128)S(1)}, u32[]{:S(2)}, u32[]{:S(2)}) collective-permute-start(f32[4,10,10,1]{3,2,1,0:T(8,128)} %get-tuple-element.76), channel_id=1, source_target_pairs={{1,0},{2,1},{3,2},{5,4},{6,5},{7,6},{9,8},{10,9},{11,10},{13,12},{... | collective-permute-start | bytes 4808 | tf_op jit(solution)/shard_map/ppermute | solution.py:49
  167.2 261.9 %collective-permute-start.19 = (f32[4,10,10,1]{3,2,1,0:T(8,128)}, f32[4,10,10,1]{3,2,1,0:T(8,128)S(1)}, u32[]{:S(2)}, u32[]{:S(2)}) collective-permute-start(f32[4,10,10,1]{3,2,1,0:T(8,128)} %get-tuple-element.77), channel_id=1, source_target_pairs={{0,1},{1,2},{2,3},{4,5},{5,6},{6,7},{8,9},{9,10},{10,11},{12,13},{... | collective-permute-start | bytes 4808 | tf_op jit(solution)/shard_map/ppermute | solution.py:47
  247.9 6.2 %collective-permute-start.4 = (f32[4,1920]{1,0:T(4,128)S(1)}, f32[4,1920]{1,0:T(4,128)S(1)}, u32[]{:S(2)}, u32[]{:S(2)}) collective-permute-start(f32[4,1920]{1,0:T(4,128)S(1)} %pad.15.clone), channel_id=1, source_target_pairs={{0,8},{8,16},{16,24},{1,9},{9,17},{17,25},{2,10},{10,18},{18,26},{... | collective-permute-start | bytes 92168 | tf_op jit(solution)/shard_map/ppermute | solution.py:47
  249.8 5.8 %collective-permute-start.5 = (f32[4,1920]{1,0:T(4,128)S(1)}, f32[4,1920]{1,0:T(4,128)S(1)}, u32[]{:S(2)}, u32[]{:S(2)}) collective-permute-start(f32[4,1920]{1,0:T(4,128)S(1)} %pad.15.clone), channel_id=1, source_target_pairs={{8,0},{16,8},{24,16},{9,1},{17,9},{25,17},{10,2},{18,10},{26,18},{... | collective-permute-start | bytes 92168 | tf_op jit(solution)/shard_map/ppermute | solution.py:49
  333.7 6.2 %collective-permute-start.6 = (f32[4,1920]{1,0:T(4,128)S(1)}, f32[4,1920]{1,0:T(4,128)S(1)}, u32[]{:S(2)}, u32[]{:S(2)}) collective-permute-start(f32[4,1920]{1,0:T(4,128)S(1)} %pad.16.clone), channel_id=1, source_target_pairs={{0,8},{8,16},{16,24},{1,9},{9,17},{17,25},{2,10},{10,18},{18,26},{... | collective-permute-start | bytes 92168 | tf_op jit(solution)/shard_map/ppermute | solution.py:47
  335.6 5.8 %collective-permute-start.7 = (f32[4,1920]{1,0:T(4,128)S(1)}, f32[4,1920]{1,0:T(4,128)S(1)}, u32[]{:S(2)}, u32[]{:S(2)}) collective-permute-start(f32[4,1920]{1,0:T(4,128)S(1)} %pad.16.clone), channel_id=1, source_target_pairs={{8,0},{16,8},{24,16},{9,1},{17,9},{25,17},{10,2},{18,10},{26,18},{... | collective-permute-start | bytes 92168 | tf_op jit(solution)/shard_map/ppermute | solution.py:49
  429.5 5.9 %collective-permute-start.20 = (f32[4,1,8,128]{3,2,1,0:T(8,128)S(1)}, f32[4,1,8,128]{3,2,1,0:T(8,128)S(1)}, u32[]{:S(2)}, u32[]{:S(2)}) collective-permute-start(f32[4,1,8,128]{3,2,1,0:T(8,128)S(1)} %get-tuple-element.202), channel_id=1, source_target_pairs={{8,0},{16,8},{24,16},{9,1},{17,9},{25,17},{10,2},{18,10},{26,18},{... | collective-permute-start | bytes 49160 | tf_op jit(solution)/shard_map/ppermute | solution.py:49
  431.4 6.5 %collective-permute-start.21 = (f32[4,1,8,128]{3,2,1,0:T(8,128)S(1)}, f32[4,1,8,128]{3,2,1,0:T(8,128)S(1)}, u32[]{:S(2)}, u32[]{:S(2)}) collective-permute-start(f32[4,1,8,128]{3,2,1,0:T(8,128)S(1)} %get-tuple-element.201), channel_id=1, source_target_pairs={{0,8},{8,16},{16,24},{1,9},{9,17},{17,25},{2,10},{10,18},{18,26},{... | collective-permute-start | bytes 49160 | tf_op jit(solution)/shard_map/ppermute | solution.py:47
  437.9 6.0 %collective-permute-start.22 = (f32[4,10,1,128]{3,2,1,0:T(1,128)S(1)}, f32[4,10,1,128]{3,2,1,0:T(1,128)S(1)}, u32[]{:S(2)}, u32[]{:S(2)}) collective-permute-start(f32[4,10,1,128]{3,2,1,0:T(1,128)S(1)} %get-tuple-element.102), channel_id=1, source_target_pairs={{4,0},{5,1},{6,2},{7,3},{12,8},{13,9},{14,10},{15,11},{20,16},{21,... | collective-permute-start | bytes 61448 | tf_op jit(solution)/shard_map/ppermute | solution.py:49
  442.5 5.7 %collective-permute-start.23 = (f32[4,10,1,128]{3,2,1,0:T(1,128)S(1)}, f32[4,10,1,128]{3,2,1,0:T(1,128)S(1)}, u32[]{:S(2)}, u32[]{:S(2)}) collective-permute-start(f32[4,10,1,128]{3,2,1,0:T(1,128)S(1)} %get-tuple-element.101), channel_id=1, source_target_pairs={{0,4},{1,5},{2,6},{3,7},{8,12},{9,13},{10,14},{11,15},{16,20},{17,... | collective-permute-start | bytes 61448 | tf_op jit(solution)/shard_map/ppermute | solution.py:47
  448.4 6.5 %collective-permute-start.24 = (f32[4,10,10,1]{3,2,1,0:T(8,128)S(1)}, f32[4,10,10,1]{3,2,1,0:T(8,128)S(1)}, u32[]{:S(2)}, u32[]{:S(2)}) collective-permute-start(f32[4,10,10,1]{3,2,1,0:T(8,128)S(1)} %get-tuple-element.74), channel_id=1, source_target_pairs={{1,0},{2,1},{3,2},{5,4},{6,5},{7,6},{9,8},{10,9},{11,10},{13,12},{... | collective-permute-start | bytes 4808 | tf_op jit(solution)/shard_map/ppermute | solution.py:49
  450.3 8.4 %collective-permute-start.25 = (f32[4,10,10,1]{3,2,1,0:T(8,128)S(1)}, f32[4,10,10,1]{3,2,1,0:T(8,128)S(1)}, u32[]{:S(2)}, u32[]{:S(2)}) collective-permute-start(f32[4,10,10,1]{3,2,1,0:T(8,128)S(1)} %get-tuple-element.75), channel_id=1, source_target_pairs={{0,1},{1,2},{2,3},{4,5},{5,6},{6,7},{8,9},{9,10},{10,11},{12,13},{... | collective-permute-start | bytes 4808 | tf_op jit(solution)/shard_map/ppermute | solution.py:47
  459.1 5.9 %collective-permute-start.26 = (f32[4,1,8,128]{3,2,1,0:T(8,128)S(1)}, f32[4,1,8,128]{3,2,1,0:T(8,128)S(1)}, u32[]{:S(2)}, u32[]{:S(2)}) collective-permute-start(f32[4,1,8,128]{3,2,1,0:T(8,128)S(1)} %get-tuple-element.200), channel_id=1, source_target_pairs={{8,0},{16,8},{24,16},{9,1},{17,9},{25,17},{10,2},{18,10},{26,18},{... | collective-permute-start | bytes 49160 | tf_op jit(solution)/shard_map/ppermute | solution.py:49
  463.0 5.6 %collective-permute-start.27 = (f32[4,1,8,128]{3,2,1,0:T(8,128)S(1)}, f32[4,1,8,128]{3,2,1,0:T(8,128)S(1)}, u32[]{:S(2)}, u32[]{:S(2)}) collective-permute-start(f32[4,1,8,128]{3,2,1,0:T(8,128)S(1)} %get-tuple-element.199), channel_id=1, source_target_pairs={{0,8},{8,16},{16,24},{1,9},{9,17},{17,25},{2,10},{10,18},{18,26},{... | collective-permute-start | bytes 49160 | tf_op jit(solution)/shard_map/ppermute | solution.py:47
  468.7 3.1 collective-permute-start.28
  470.3 5.7 %collective-permute-start.29 = (f32[4,10,1,128]{3,2,1,0:T(1,128)S(1)}, f32[4,10,1,128]{3,2,1,0:T(1,128)S(1)}, u32[]{:S(2)}, u32[]{:S(2)}) collective-permute-start(f32[4,10,1,128]{3,2,1,0:T(1,128)S(1)} %get-tuple-element.100), channel_id=1, source_target_pairs={{0,4},{1,5},{2,6},{3,7},{8,12},{9,13},{10,14},{11,15},{16,20},{17,... | collective-permute-start | bytes 61448 | tf_op jit(solution)/shard_map/ppermute | solution.py:47
  476.2 6.5 %collective-permute-start.30 = (f32[4,10,10,1]{3,2,1,0:T(8,128)S(1)}, f32[4,10,10,1]{3,2,1,0:T(8,128)S(1)}, u32[]{:S(2)}, u32[]{:S(2)}) collective-permute-start(f32[4,10,10,1]{3,2,1,0:T(8,128)S(1)} %get-tuple-element.72), channel_id=1, source_target_pairs={{1,0},{2,1},{3,2},{5,4},{6,5},{7,6},{9,8},{10,9},{11,10},{13,12},{... | collective-permute-start | bytes 4808 | tf_op jit(solution)/shard_map/ppermute | solution.py:49
  478.1 8.4 %collective-permute-start.31 = (f32[4,10,10,1]{3,2,1,0:T(8,128)S(1)}, f32[4,10,10,1]{3,2,1,0:T(8,128)S(1)}, u32[]{:S(2)}, u32[]{:S(2)}) collective-permute-start(f32[4,10,10,1]{3,2,1,0:T(8,128)S(1)} %get-tuple-element.73), channel_id=1, source_target_pairs={{0,1},{1,2},{2,3},{4,5},{5,6},{6,7},{8,9},{9,10},{10,11},{12,13},{... | collective-permute-start | bytes 4808 | tf_op jit(solution)/shard_map/ppermute | solution.py:47
  (34 other events, 734.7 us)
where the time goes:
time: 496 us; the launch traced here: 488 us
  local copies, waits for them, and re-layouts  326 us (66%)
  starting transfers between devices  83.7 us (17%)
  waiting for transfers between devices  32.8 us (7%)
  other arithmetic  17.8 us (4%)
  blocking collectives  14.7 us (3%)
  matrix products  7.84 us (2%)
  between operations  4.97 us (1%)
    gather x8, local copies, waits for them, and re-layouts, shards(): arrived = jnp.where(valid, jnp.take(extended.reshape(-1), flat_index), 0.0)  159 us
    gather x144, local copies, waits for them, and re-layouts, stream(): jnp.take(pool, jnp.asarray(tables['selects'][member], jnp.int32), axis=1)  82.6 us
    ppermute x16, starting transfers between devices, padded(): lax.ppermute(head, axis, [((i + 1) % count, i) for i in range(ends)])  46.6 us
    ppermute x16, starting transfers between devices, padded(): lax.ppermute(tail, axis, [(i, (i + 1) % count) for i in range(ends)])  37.1 us
    gather x4, local copies, waits for them, and re-layouts, rim_rows(): rim = jnp.take(flat, jnp.asarray(tables['rim_source'], jnp.int32), axis=1)  23.3 us
    ppermute x16, waiting for transfers between devices, padded(): lax.ppermute(tail, axis, [(i, (i + 1) % count) for i in range(ends)])  22.4 us
    gather x36, local copies, waits for them, and re-layouts, stream(): jnp.take(beside_ids, jnp.asarray(tables['dir_maps'][member], jnp.int32),...  20.7 us
    all_gather x1, blocking collectives, shards(): lax.all_gather(part, 'gx', axis=0, tiled=True)  14.7 us
  transfers between devices with their start and end apart: 32, of which 13 were waited for; matrix products, arithmetic and copies ran while one was open for 69% of the time, Pallas kernels for 0%

commit v1 on v0

--- a/solution.py
+++ b/solution.py
@@ -2,6 +2,8 @@
 import jax.numpy as jnp
 import numpy as np
 from jax import lax
+from jax.experimental import pallas as pl
+from jax.experimental.pallas import tpu as pltpu
 from jax.sharding import PartitionSpec as P
 
 FLOW_STEPS = 4
@@ -279,9 +281,498 @@
     return (weighted, conc)
 
 
+MESH = pl.DeviceIdType.MESH
+AXES = ("gx", "gy", "gz")
+CHUNKS = 2
+
+
+def iota(axis):
+    return lax.broadcasted_iota(jnp.int32, (8, 128), axis)
+
+
+def take(values, index, axis):
+    return jnp.take_along_axis(values, index, axis=axis, mode="promise_in_bounds")
+
+
+def swap_indices():
+    row, lane = iota(0), iota(1)
+    half, group, cell = lane // 64, (lane // 8) % 8, lane % 8
+    ahead = half * 64 + ((group + row) % 8) * 8 + cell
+    rows = (row - group + 8) % 8
+    back = half * 64 + rows * 8 + cell
+    return ahead, rows, back
+
+
+def swap(values, indices):
+    ahead, rows, back = indices
+    return take(take(take(values, ahead, 1), rows, 0), back, 1)
+
+
+def tables_needed():
+    keys = []
+    for vec in LATTICE_DIRS[1:]:
+        for face_x in {0, -vec[0]}:
+            for face_y in {0, -vec[1]}:
+                key = (face_x, face_y, vec[2])
+                if key != (0, 0, 0) and key not in keys:
+                    keys.append(key)
+    return sorted(keys)
+
+
+TABLE_KEYS = tables_needed()
+
+
+def weight_of(member):
+    return 1.0 / 3.0 if member == 0 else (1.0 / 18.0 if member < 7 else 1.0 / 36.0)
+
+
+def moments(popul):
+    density = popul[0]
+    momentum = [None, None, None]
+    for member in range(1, 19):
+        density = density + popul[member]
+        for axis in range(3):
+            sign = LATTICE_DIRS[member][axis]
+            if sign:
+                term = popul[member]
+                if momentum[axis] is None:
+                    momentum[axis] = term if sign > 0 else -term
+                else:
+                    momentum[axis] = momentum[axis] + term if sign > 0 else momentum[axis] - term
+    return density, momentum
+
+
+def relaxed(popul, density, momentum, relax):
+    square = momentum[0] * momentum[0] + momentum[1] * momentum[1] + momentum[2] * momentum[2]
+    rest = density - 1.5 * square
+    result = [popul[0] - relax * (popul[0] - rest * (1.0 / 3.0))]
+    for member in range(1, 19, 2):
+        vec = LATTICE_DIRS[member]
+        weight = weight_of(member)
+        project = None
+        for axis in range(3):
+            if vec[axis]:
+                term = momentum[axis]
+                if project is None:
+                    project = term if vec[axis] > 0 else -term
+                else:
+                    project = project + term if vec[axis] > 0 else project - term
+        even = weight * rest + (4.5 * weight) * (project * project)
+        odd = (3.0 * weight) * project
+        result.append(popul[member] - relax * (popul[member] - (even + odd)))
+        result.append(popul[member + 1] - relax * (popul[member + 1] - (even - odd)))
+    return result
+
+
+def sides_of(axis):
+    count = lax.axis_size(axis)
+    here = lax.axis_index(axis)
+    return (
+        (here > 0, {axis: lax.max(here - 1, 0)}),
+        (here < count - 1, {axis: lax.min(here + 1, count - 1)}),
+    )
+
+
+def kernel(
+    pops, visc, links, flags, beside, owners, slots, conc, diff, uptake,
+    weighted, conc_out,
+    gathered, fields, post, tables, open_bits, relax_by, marks,
+    cells, rates, winds, halo_x, halo_y, halo_z, pack_y, pack_z,
+    send_g, recv_g, send_t, recv_t,
+):
+    count = lax.axis_size("gx")
+    here = lax.axis_index("gx")
+    block_count = pops.shape[1]
+    species = conc.shape[0]
+    planes = gathered.shape[1]
+    lane, row = iota(1), iota(0)
+    block_lane, cell_lane = lane // 8, lane % 8
+    halos = (halo_x, halo_y, halo_z)
+
+    for at, axis in enumerate(AXES):
+        for side, (there, _) in enumerate(sides_of(axis)):
+
+            @pl.when(jnp.logical_not(there))
+            def _(at=at, side=side):
+                for turn in range(TISSUE_STEPS):
+                    halos[at][turn, side] = jnp.zeros(halos[at].shape[2:], jnp.float32)
+
+    gathered[here, 0:19] = pops[...]
+    gathered[here, 19] = visc[...]
+    gathered[here, 20] = links[...].astype(jnp.float32)
+    gathered[here, 21] = flags[...].astype(jnp.float32)
+    gathered[here, 22] = jnp.zeros((block_count, 512), jnp.float32)
+    gathered[here, 22, :, 0:18] = beside[...].astype(jnp.float32)
+    for kind in range(species):
+        cells[0, kind] = conc[kind]
+    cells[0, species] = diff[...]
+
+    def pack(slot, turn):
+        kinds = species + 1 if turn == 0 else species
+        for side, spot in ((0, 0), (1, 7)):
+            zcol = 0 if side == 0 else 127
+            packed = jnp.zeros((8, 128), jnp.float32)
+            for kind in range(kinds):
+                for a in range(8):
+                    tile = cells[slot, kind, a]
+                    pack_y[turn, side, kind, a : a + 1] = tile[spot : spot + 1]
+                    packed = jnp.where(
+                        lane == kind * 8 + a,
+                        jnp.broadcast_to(tile[:, zcol : zcol + 1], (8, 128)),
+                        packed,
+                    )
+            pack_z[turn, side] = packed
+
+    def face_copy(slot, turn, at, side, device, landing):
+        kinds = species + 1 if turn == 0 else species
+        if at == 0:
+            source = cells.at[slot, pl.ds(0, kinds), 0 if side == 0 else 7]
+            target = halo_x.at[turn, landing, pl.ds(0, kinds)]
+        elif at == 1:
+            source = pack_y.at[turn, side, pl.ds(0, kinds)]
+            target = halo_y.at[turn, landing, pl.ds(0, kinds)]
+        else:
+            source = pack_z.at[turn, side]
+            target = halo_z.at[turn, landing]
+        return pltpu.make_async_remote_copy(
+            src_ref=source,
+            dst_ref=target,
+            send_sem=send_t.at[turn, at * 2 + side],
+            recv_sem=recv_t.at[turn, at * 2 + landing],
+            device_id=device,
+            device_id_type=MESH,
+        )
+
+    def start_faces(slot, turn):
+        pack(slot, turn)
+        for at, axis in enumerate(AXES):
+            for side, (there, device) in enumerate(sides_of(axis)):
+
+                @pl.when(there)
+                def _(at=at, side=side, device=device):
+                    face_copy(slot, turn, at, side, device, 1 - side).start()
+
+    def wait_faces(slot, turn):
+        for at, axis in enumerate(AXES):
+            for side, (there, device) in enumerate(sides_of(axis)):
+
+                @pl.when(there)
+                def _(at=at, side=side, device=device):
+                    face_copy(slot, turn, at, side, device, 1 - side).wait_send()
+                    face_copy(slot, turn, at, side, device, side).wait_recv()
+
+    barrier = pltpu.get_barrier_semaphore()
+    expected = 0
+    for axis in AXES:
+        for there, device in sides_of(axis):
+
+            @pl.when(there)
+            def _(device=device):
+                pl.semaphore_signal(barrier, inc=1, device_id=device, device_id_type=MESH)
+
+            expected = expected + there.astype(jnp.int32)
+    pl.semaphore_wait(barrier, expected)
+
+    bounds = [planes * part // CHUNKS for part in range(CHUNKS + 1)]
+    neighbours = sides_of("gx")
+
+    def slab_copy(owner, way, hop, part, device):
+        view = gathered.at[owner, pl.ds(bounds[part], bounds[part + 1] - bounds[part])]
+        return pltpu.make_async_remote_copy(
+            src_ref=view,
+            dst_ref=view,
+            send_sem=send_g.at[way, hop, part],
+            recv_sem=recv_g.at[way, hop, part],
+            device_id=device,
+            device_id_type=MESH,
+        )
+
+    def slab_of(way, hop):
+        owner = here - hop if way == 1 else here + hop
+        valid = owner >= 0 if way == 1 else owner < count
+        return lax.clamp(0, owner, count - 1), valid
+
+    for hop in range(count):
+        for part in range(CHUNKS):
+            for way in range(2):
+                owner, valid = slab_of(way, hop)
+                there, device = neighbours[way]
+                back_device = neighbours[1 - way][1]
+                if hop > 0:
+
+                    @pl.when(valid)
+                    def _(owner=owner, way=way, hop=hop, part=part, device=back_device):
+                        slab_copy(owner, way, hop - 1, part, device).wait_recv()
+
+                if hop < count - 1:
+
+                    @pl.when(jnp.logical_and(valid, there))
+                    def _(owner=owner, way=way, hop=hop, part=part, device=device):
+                        slab_copy(owner, way, hop, part, device).start()
+
+        if hop == 0:
+            start_faces(0, 0)
+
+    for hop in range(count - 1):
+        for part in range(CHUNKS):
+            for way in range(2):
+                owner, valid = slab_of(way, hop)
+                there, device = neighbours[way]
+
+                @pl.when(jnp.logical_and(valid, there))
+                def _(owner=owner, way=way, hop=hop, part=part, device=device):
+                    slab_copy(owner, way, hop, part, device).wait_send()
+
+    indices = swap_indices()
+    low = lane < 64
+
+    def arrange(plane, carry):
+        for tile in range(4):
+            cut = pl.ds(tile * 128, 128)
+            first = jnp.concatenate([gathered[0, plane, :, cut], gathered[1, plane, :, cut]], axis=0)
+            second = jnp.concatenate([gathered[2, plane, :, cut], gathered[3, plane, :, cut]], axis=0)
+            even = jnp.where(low, first, pltpu.roll(second, 64, 1))
+            odd = jnp.where(low, pltpu.roll(first, 64, 1), second)
+            fields[plane, 2 * tile] = swap(even, indices)
+            fields[plane, 2 * tile + 1] = swap(odd, indices)
+        return carry
+
+    lax.fori_loop(0, 22, arrange, 0)
+
+    ids = jnp.concatenate([gathered[dev, 22, :, 0:128] for dev in range(4)], axis=0)
+    ids = jnp.concatenate([ids, jnp.zeros((112, 128), jnp.float32)], axis=0)
+    spread = lax.broadcasted_iota(jnp.int32, (128, 128), 1) // 8
+    spread = (spread == lax.broadcasted_iota(jnp.int32, (128, 128), 0)).astype(jnp.float32)
+    by_dir = lax.dot_general(
+        ids, spread, (((0,), (0,)), ((), ())), preferred_element_type=jnp.float32
+    )
+
+    def beside_of(vec):
+        at = LATTICE_DIRS.index(vec) - 1
+        return jnp.broadcast_to(by_dir[at : at + 1], (8, 128)).astype(jnp.int32)
+
+    has = {(0, 0, 0): jnp.ones((8, 128), jnp.int32)}
+    for at, (face_x, face_y, step) in enumerate(TABLE_KEYS):
+        inner = block_lane if face_x == 0 and face_y == 0 else beside_of((face_x, face_y, 0))
+        cell = cell_lane
+        if step:
+            crossing = cell_lane == (0 if step > 0 else 7)
+            inner = jnp.where(crossing, beside_of((face_x, face_y, -step)), inner)
+            cell = (cell_lane - step + 8) % 8
+        tables[at] = jnp.clip(inner, 0, 15) * 8 + cell
+        has[face_x, face_y, step] = jnp.where(inner >= 0, 1, 0)
+
+    def row_face(vec):
+        return row == (0 if vec[1] > 0 else 7)
+
+    for a in range(8):
+        bits = fields[20, a].astype(jnp.int32)
+        allowed = jnp.zeros((8, 128), jnp.int32)
+        for member in range(1, 19):
+            vec = LATTICE_DIRS[member]
+            face_x = -vec[0] if not 0 <= a - vec[0] <= 7 else 0
+            usable = has[face_x, 0, vec[2]]
+            if vec[1]:
+                usable = jnp.where(row_face(vec), has[face_x, -vec[1], vec[2]], usable)
+            allowed = allowed + usable * (1 << (member - 1))
+        open_bits[a] = bits & allowed
+        flagged = fields[21, a]
+        relax = 1.0 / (3.0 * fields[19, a] + 0.5)
+        inside = flagged < 0.5
+        relax_by[0, a] = jnp.where(inside, relax, 1.0)
+        relax_by[1, a] = jnp.where(inside, 0.0, 1.0)
+        marks[a] = jnp.where(
+            inside, 0.0, jnp.where(flagged < 1.5, INLET_DENSITY, OUTLET_DENSITY)
+        )
+
+    def first_collision(a, carry):
+        popul = [fields[member, a] * weight_of(member) for member in range(19)]
+        density, momentum = moments(popul)
+        relax = 1.0 / (3.0 * fields[19, a] + 0.5)
+        for member, value in enumerate(relaxed(popul, density, momentum, relax)):
+            post[0, member, a] = value
+        return carry
+
+    lax.fori_loop(0, 8, first_collision, 0)
+
+    def flow_step(turn, carry):
+        now = lax.rem(turn, 2)
+        later = 1 - now
+        final = jnp.where(turn == FLOW_STEPS - 1, 1, 0)
+        for a in range(8):
+            bits = open_bits[a]
+            popul = [post[now, 0, a]]
+            for member in range(1, 19):
+                vec = LATTICE_DIRS[member]
+                opposite = member + 1 if member % 2 else member - 1
+                from_a = a - vec[0]
+                face_x = 0 if 0 <= from_a <= 7 else -vec[0]
+                source = post[now, member, from_a % 8]
+                if vec[1]:
+                    source = pltpu.roll(source, vec[1] % 8, 0)
+                pulled = source
+                key = (face_x, 0, vec[2])
+                if key != (0, 0, 0):
+                    pulled = take(source, tables[TABLE_KEYS.index(key)], 1)
+                if vec[1]:
+                    key = (face_x, -vec[1], vec[2])
+                    other = take(source, tables[TABLE_KEYS.index(key)], 1)
+                    pulled = jnp.where(row_face(vec), other, pulled)
+                closed = (bits & (1 << (member - 1))) == 0
+                popul.append(jnp.where(closed, post[now, opposite, a], pulled))
+            density, momentum = moments(popul)
+            mark = marks[a]
+            density = jnp.where(mark > 0.0, mark, density)
+            for member, value in enumerate(relaxed(popul, density, momentum, relax_by[final, a])):
+                post[later, member, a] = value
+        return carry
+
+    lax.fori_loop(0, FLOW_STEPS, flow_step, 0)
+    last = FLOW_STEPS % 2
+
+    source_lane = jnp.full((8, 128), -1, jnp.int32)
+    for block in range(16):
+        owner_here = jnp.broadcast_to(owners[:, block : block + 1], (8, 128))
+        slot_here = jnp.broadcast_to(slots[:, block : block + 1], (8, 128))
+        hit = (owner_here == here) & (slot_here == block_lane)
+        source_lane = jnp.where(hit, block * 8 + cell_lane, source_lane)
+    filled = source_lane >= 0
+    source_lane = jnp.maximum(source_lane, 0)
+    for a in range(8):
+        _, momentum = moments([post[last, member, a] for member in range(19)])
+        for axis in range(3):
+            speed = ADVECT_GAIN * jnp.where(filled, take(momentum[axis], source_lane, 1), 0.0)
+            winds[2 * axis, a] = jnp.maximum(speed, 0.0)
+            winds[2 * axis + 1, a] = -jnp.minimum(speed, 0.0)
+
+    def beside_cells(slot, turn, kind, a):
+        center = cells[slot, kind, a]
+        result = []
+        result.append(halo_x[turn, 0, kind] if a == 0 else cells[slot, kind, a - 1])
+        result.append(halo_x[turn, 1, kind] if a == 7 else cells[slot, kind, a + 1])
+        for side, spot in ((0, 0), (1, 7)):
+            edge = jnp.broadcast_to(halo_y[turn, side, kind, a : a + 1], (8, 128))
+            result.append(jnp.where(row == spot, edge, pltpu.roll(center, 1 if side == 0 else 7, 0)))
+        for side, spot in ((0, 0), (1, 127)):
+            col = kind * 8 + a
+            edge = jnp.broadcast_to(halo_z[turn, side, :, col : col + 1], (8, 128))
+            result.append(jnp.where(lane == spot, edge, pltpu.roll(center, 1 if side == 0 else 127, 1)))
+        return center, result
+
+    def tissue(slot, turn):
+        for a in range(8):
+            if turn == 0:
+                center, around = beside_cells(0, 0, species, a)
+                for way in range(6):
+                    rates[way, a] = 0.5 * (center + around[way])
+            rate = [rates[way, a] for way in range(6)]
+            wind = [winds[way, a] for way in range(6)]
+            appetite = uptake[a]
+            eaten = None
+            for kind in range(species):
+                center, around = beside_cells(slot, turn, kind, a)
+                total = center
+                for way in range(6):
+                    gain = DIFFUSION_GAIN[kind] * rate[way] + wind[way]
+                    total = total + gain * (around[way] - center)
+                if kind != 2:
+                    eaten_here = appetite * center / (HALF_SATURATION[kind] + jnp.abs(center))
+                    total = total - eaten_here
+                    if kind == 1:
+                        eaten = eaten_here
+                else:
+                    total = total + 2.0 * eaten
+                if turn == TISSUE_STEPS - 1:
+                    conc_out[kind, a] = total
+                else:
+                    cells[1 - slot, kind, a] = total
+
+    upper = here * block_count >= 8
+    shift_rows = lax.rem(here * block_count, 8) > 0
+
+    def hand_out(member, carry):
+        scale = jnp.where(member == 0, 3.0, jnp.where(member < 7, 18.0, 36.0))
+        for tile in range(4):
+            even = post[last, member, 2 * tile]
+            odd = post[last, member, 2 * tile + 1]
+            lower_part = jnp.where(low, even, pltpu.roll(odd, 64, 1))
+            upper_part = jnp.where(low, pltpu.roll(even, 64, 1), odd)
+            rows = swap(jnp.where(upper, upper_part, lower_part), indices) * scale
+            rows = jnp.where(shift_rows, pltpu.roll(rows, 4, 0), rows)
+            weighted[member, :, pl.ds(tile * 128, 128)] = rows[0:4]
+        return carry
+
+    for turn in range(TISSUE_STEPS):
+        slot = turn % 2
+        if turn > 0:
+            start_faces(slot, turn)
+            middle = 19 * turn // (TISSUE_STEPS - 1)
+            lax.fori_loop(19 * (turn - 1) // (TISSUE_STEPS - 1), middle, hand_out, 0)
+        wait_faces(slot, turn)
+        tissue(slot, turn)
+
+
+def fused(
+    populations, viscosity, links, flags, neighbours, owners, slots,
+    concentrations, diffusivity, uptake_rate,
+):
+    count = lax.axis_size("gx")
+    block_count = populations.shape[2]
+    species = concentrations.shape[0]
+    vmem = pl.BlockSpec(memory_space=pltpu.VMEM)
+    f32 = jnp.float32
+    weighted, conc = pl.pallas_call(
+        kernel,
+        out_shape=(
+            jax.ShapeDtypeStruct((19, block_count, 512), f32),
+            jax.ShapeDtypeStruct(concentrations.shape, f32),
+        ),
+        in_specs=[vmem] * 10,
+        out_specs=(vmem, vmem),
+        scratch_shapes=[
+            pltpu.VMEM((count, 23, block_count, 512), f32),
+            pltpu.VMEM((22, 8, 8, 128), f32),
+            pltpu.VMEM((2, 19, 8, 8, 128), f32),
+            pltpu.VMEM((len(TABLE_KEYS), 8, 128), jnp.int32),
+            pltpu.VMEM((8, 8, 128), jnp.int32),
+            pltpu.VMEM((2, 8, 8, 128), f32),
+            pltpu.VMEM((8, 8, 128), f32),
+            pltpu.VMEM((2, species + 1, 8, 8, 128), f32),
+            pltpu.VMEM((6, 8, 8, 128), f32),
+            pltpu.VMEM((6, 8, 8, 128), f32),
+            pltpu.VMEM((TISSUE_STEPS, 2, species + 1, 8, 128), f32),
+            pltpu.VMEM((TISSUE_STEPS, 2, species + 1, 8, 128), f32),
+            pltpu.VMEM((TISSUE_STEPS, 2, 8, 128), f32),
+            pltpu.VMEM((TISSUE_STEPS, 2, species + 1, 8, 128), f32),
+            pltpu.VMEM((TISSUE_STEPS, 2, 8, 128), f32),
+            pltpu.SemaphoreType.DMA((2, count - 1, CHUNKS)),
+            pltpu.SemaphoreType.DMA((2, count - 1, CHUNKS)),
+            pltpu.SemaphoreType.DMA((TISSUE_STEPS, 6)),
+            pltpu.SemaphoreType.DMA((TISSUE_STEPS, 6)),
+        ],
+        compiler_params=pltpu.CompilerParams(
+            collective_id=0, has_side_effects=True, vmem_limit_bytes=32 * 1024 * 1024
+        ),
+    )(
+        populations[:, 0], viscosity[0], links[0], flags[0], neighbours[0], owners, slots,
+        concentrations, diffusivity, uptake_rate,
+    )
+    return weighted[:, None], conc
+
+
+def per_device(*arrays):
+    populations, concentrations = arrays[0], arrays[7]
+    fits = (
+        lax.axis_size("gx") == 4
+        and populations.shape[2] == 4
+        and concentrations.shape[1:] == (8, 8, 128)
+    )
+    return fused(*arrays) if fits else shards(*arrays)
+
+
 def solution(mesh):
     return jax.shard_map(
-        shards,
+        per_device,
         mesh=mesh,
         in_specs=(
             P(None, ("gy", "gz"), "gx", None),

time: 496 us -> 43.7 us (0.09)
  the two profiles are of different devices: /device:TPU:22 before, /device:TPU:0 now
where the time goes in v1:
time: 43.7 us; the launch traced here: 43.3 us
  Pallas kernels  35.2 us (81%)
  local copies, waits for them, and re-layouts  7.4 us (17%)
  between operations  0.67 us (2%)
    pallas_call x1, Pallas kernels, fused(): pl.pallas_call(kernel, out_shape=(jax.ShapeDtypeStruct((19, block_count,...  35.2 us
    unnamed x22, local copies, waits for them, and re-layouts  7.4 us

profile of v1, /device:TPU:0, one launch (start us, length us, event | category | flops | bytes accessed | tf_op | source)
XLA Modules:
  0.0 43.3 jit_solution(10222005150844849452)
XLA Ops:
  0.6 0.0 copy-start.4
  0.6 0.0 copy-start.8
  0.7 0.0 copy-start.9
  0.7 0.7 %copy-done.4 = f32[1,4,512]{2,1,0:T(4,128)S(1)} copy-done((f32[1,4,512]{2,1,0:T(4,128)S(1)}, f32[1,4,512]{2,1,0:T(4,128)}, u32[]{:S(2)}) %copy-start.4) | copy-done | bytes 8216
  1.3 0.0 copy-done.8
  1.3 0.0 copy-done.9
  1.3 0.0 copy-start
  1.3 0.9 %copy-done = f32[19,1,4,512]{3,2,1,0:T(4,128)S(1)} copy-done((f32[19,1,4,512]{3,2,1,0:T(4,128)S(1)}, f32[19,1,4,512]{3,2,1,0:T(4,128)}, u32[]{:S(2)}) %copy-start) | copy-done | bytes 155672
  2.3 0.0 copy-start.1
  2.3 0.9 %copy-done.1 = f32[4,8,8,128]{3,2,1,0:T(8,128)S(1)} copy-done((f32[4,8,8,128]{3,2,1,0:T(8,128)S(1)}, f32[4,8,8,128]{3,2,1,0:T(8,128)}, u32[]{:S(2)}) %copy-start.1) | copy-done | bytes 131096
  3.2 0.0 copy-start.2
  3.2 0.8 %copy-done.2 = f32[8,8,128]{2,1,0:T(8,128)S(1)} copy-done((f32[8,8,128]{2,1,0:T(8,128)S(1)}, f32[8,8,128]{2,1,0:T(8,128)}, u32[]{:S(2)}) %copy-start.2) | copy-done | bytes 32792
  3.9 0.0 copy-start.3
  3.9 0.8 %copy-done.3 = f32[8,8,128]{2,1,0:T(8,128)S(1)} copy-done((f32[8,8,128]{2,1,0:T(8,128)S(1)}, f32[8,8,128]{2,1,0:T(8,128)}, u32[]{:S(2)}) %copy-start.3) | copy-done | bytes 32792
  4.7 0.0 copy-start.5
  4.7 0.7 %copy-done.5 = s32[1,4,512]{2,1,0:T(4,128)S(1)} copy-done((s32[1,4,512]{2,1,0:T(4,128)S(1)}, s32[1,4,512]{2,1,0:T(4,128)}, u32[]{:S(2)}) %copy-start.5) | copy-done | bytes 8216
  5.4 0.0 copy-start.6
  5.4 0.7 %copy-done.6 = s32[1,4,512]{2,1,0:T(4,128)S(1)} copy-done((s32[1,4,512]{2,1,0:T(4,128)S(1)}, s32[1,4,512]{2,1,0:T(4,128)}, u32[]{:S(2)}) %copy-start.6) | copy-done | bytes 8216
  6.1 0.0 copy-start.7
  6.1 0.7 %copy-done.7 = s32[1,4,18]{2,1,0:T(4,128)S(1)} copy-done((s32[1,4,18]{2,1,0:T(4,128)S(1)}, s32[1,4,18]{2,1,0:T(4,128)}, u32[]{:S(2)}) %copy-start.7) | copy-done | bytes 312
  6.7 35.2 %shard_map.113 = (f32[19,4,512]{2,1,0:T(4,128)S(1)}, f32[4,8,8,128]{3,2,1,0:T(8,128)S(1)}) custom-call(f32[19,4,512]{2,1,0:T(4,128)S(1)} %bitcast.8, f32[4,512]{1,0:T(4,128)S(1)} %bitcast.10, s32[4,512]{1,0:T(4,128)S(1)} %bitcast.11, s32[4,512]{1,0:T(4,128)S(1)} %bitcast.12, s32[4,18]{1,0:T(4,128)S(1)} %bitcast.13, s32[1,16]{1,0:T(1,128)S(1)} %copy-done.8, ...), custom_call_target="tpu_custom_call" | custom-call | tf_op jit(solution)/shard_map/pallas_call | solution.py:724
  42.0 0.7 %copy.15 = f32[19,1,4,512]{3,2,1,0:T(4,128)} copy(f32[19,1,4,512]{3,2,1,0:T(4,128)S(1)} %bitcast.9) | data formatting | bytes 311296
  42.6 0.7 %copy.16 = f32[4,8,8,128]{3,2,1,0:T(8,128)} copy(f32[4,8,8,128]{3,2,1,0:T(8,128)S(1)} %get-tuple-element.11) | data formatting | bytes 262144
Async XLA Ops:
  0.6 0.7 %copy-start.4 = (f32[1,4,512]{2,1,0:T(4,128)S(1)}, f32[1,4,512]{2,1,0:T(4,128)}, u32[]{:S(2)}) copy-start(f32[1,4,512]{2,1,0:T(4,128)} %param.11) | copy-start | bytes 24580
  0.6 0.7 %copy-start.8 = (s32[1,16]{1,0:T(1,128)S(1)}, s32[1,16]{1,0:T(1,128)}, u32[]{:S(2)}) copy-start(s32[1,16]{1,0:T(1,128)} %owners.1) | copy-start | bytes 196
  0.7 0.7 %copy-start.9 = (s32[1,16]{1,0:T(1,128)S(1)}, s32[1,16]{1,0:T(1,128)}, u32[]{:S(2)}) copy-start(s32[1,16]{1,0:T(1,128)} %slots.1) | copy-start | bytes 196
  1.3 0.9 %copy-start = (f32[19,1,4,512]{3,2,1,0:T(4,128)S(1)}, f32[19,1,4,512]{3,2,1,0:T(4,128)}, u32[]{:S(2)}) copy-start(f32[19,1,4,512]{3,2,1,0:T(4,128)} %param.10) | copy-start | bytes 466948
  2.3 0.9 %copy-start.1 = (f32[4,8,8,128]{3,2,1,0:T(8,128)S(1)}, f32[4,8,8,128]{3,2,1,0:T(8,128)}, u32[]{:S(2)}) copy-start(f32[4,8,8,128]{3,2,1,0:T(8,128)} %conc.1) | copy-start | bytes 393220
  3.2 0.8 %copy-start.2 = (f32[8,8,128]{2,1,0:T(8,128)S(1)}, f32[8,8,128]{2,1,0:T(8,128)}, u32[]{:S(2)}) copy-start(f32[8,8,128]{2,1,0:T(8,128)} %diff.1) | copy-start | bytes 98308
  3.9 0.8 %copy-start.3 = (f32[8,8,128]{2,1,0:T(8,128)S(1)}, f32[8,8,128]{2,1,0:T(8,128)}, u32[]{:S(2)}) copy-start(f32[8,8,128]{2,1,0:T(8,128)} %uptake.1) | copy-start | bytes 98308
  4.7 0.7 %copy-start.5 = (s32[1,4,512]{2,1,0:T(4,128)S(1)}, s32[1,4,512]{2,1,0:T(4,128)}, u32[]{:S(2)}) copy-start(s32[1,4,512]{2,1,0:T(4,128)} %param.12) | copy-start | bytes 24580
  5.4 0.7 %copy-start.6 = (s32[1,4,512]{2,1,0:T(4,128)S(1)}, s32[1,4,512]{2,1,0:T(4,128)}, u32[]{:S(2)}) copy-start(s32[1,4,512]{2,1,0:T(4,128)} %param.13) | copy-start | bytes 24580
  6.1 0.7 %copy-start.7 = (s32[1,4,18]{2,1,0:T(4,128)S(1)}, s32[1,4,18]{2,1,0:T(4,128)}, u32[]{:S(2)}) copy-start(s32[1,4,18]{2,1,0:T(4,128)} %param.14) | copy-start | bytes 868

commit v2 on v1

--- a/solution.py
+++ b/solution.py
@@ -374,11 +374,11 @@
 
 
 def kernel(
-    pops, visc, links, flags, beside, owners, slots, conc, diff, uptake,
+    pops, visc, links, flags, beside, owners_in, slots_in, conc, diff, uptake_in,
     weighted, conc_out,
-    gathered, fields, post, tables, open_bits, relax_by, marks,
+    links_at, flags_at, beside_at, owners, slots, uptake, gathered, fields, post, tables, open_bits, relax_by, marks,
     cells, rates, winds, halo_x, halo_y, halo_z, pack_y, pack_z,
-    send_g, recv_g, send_t, recv_t,
+    load, send_g, recv_g, send_t, recv_t,
 ):
     count = lax.axis_size("gx")
     here = lax.axis_index("gx")
@@ -389,6 +389,22 @@
     block_lane, cell_lane = lane // 8, lane % 8
     halos = (halo_x, halo_y, halo_z)
 
+    pairs = (
+        (pops, gathered.at[here, pl.ds(0, 19)]),
+        (visc, gathered.at[here, 19]),
+        (links, links_at),
+        (flags, flags_at),
+        (beside, beside_at),
+        (conc, cells.at[0, pl.ds(0, species)]),
+        (diff, cells.at[0, species]),
+        (uptake_in, uptake),
+        (owners_in, owners),
+        (slots_in, slots),
+    )
+    loads = [pltpu.make_async_copy(src, dst, load.at[at]) for at, (src, dst) in enumerate(pairs)]
+    for copy in loads:
+        copy.start()
+
     for at, axis in enumerate(AXES):
         for side, (there, _) in enumerate(sides_of(axis)):
 
@@ -396,16 +412,6 @@
             def _(at=at, side=side):
                 for turn in range(TISSUE_STEPS):
                     halos[at][turn, side] = jnp.zeros(halos[at].shape[2:], jnp.float32)
-
-    gathered[here, 0:19] = pops[...]
-    gathered[here, 19] = visc[...]
-    gathered[here, 20] = links[...].astype(jnp.float32)
-    gathered[here, 21] = flags[...].astype(jnp.float32)
-    gathered[here, 22] = jnp.zeros((block_count, 512), jnp.float32)
-    gathered[here, 22, :, 0:18] = beside[...].astype(jnp.float32)
-    for kind in range(species):
-        cells[0, kind] = conc[kind]
-    cells[0, species] = diff[...]
 
     def pack(slot, turn):
         kinds = species + 1 if turn == 0 else species
@@ -471,6 +477,12 @@
                 pl.semaphore_signal(barrier, inc=1, device_id=device, device_id_type=MESH)
 
             expected = expected + there.astype(jnp.int32)
+    for copy in loads[:5]:
+        copy.wait()
+    gathered[here, 20] = links_at[...].astype(jnp.float32)
+    gathered[here, 21] = flags_at[...].astype(jnp.float32)
+    gathered[here, 22] = jnp.zeros((block_count, 512), jnp.float32)
+    gathered[here, 22, :, 0:18] = beside_at[...].astype(jnp.float32)
     pl.semaphore_wait(barrier, expected)
 
     bounds = [planes * part // CHUNKS for part in range(CHUNKS + 1)]
@@ -492,6 +504,40 @@
         valid = owner >= 0 if way == 1 else owner < count
         return lax.clamp(0, owner, count - 1), valid
 
+    indices = swap_indices()
+    ahead, rows, _ = indices
+    spots = [
+        [half * 64 + ((row - 4 * late - block_lane % block_count + 16) % 8) * 8 + cell_lane
+         for half in range(2)]
+        for late in range(2)
+    ]
+
+    def absorb(owner, first):
+        mine = lane // (8 * block_count) == owner
+
+        def one(plane):
+            for pair in range(2):
+                both = jnp.concatenate(
+                    [gathered[owner, plane, :, pl.ds((2 * pair + late) * 128, 128)]
+                     for late in range(2)],
+                    axis=0,
+                )
+                both = take(take(both, ahead, 1), rows, 0)
+                for late in range(2):
+                    for half in range(2):
+                        a = 2 * (2 * pair + late) + half
+                        moved = take(both, spots[late][half], 1)
+                        if not first:
+                            moved = jnp.where(mine, moved, fields[plane, a])
+                        fields[plane, a] = moved
+
+        def two(at, carry):
+            one(2 * at)
+            one(2 * at + 1)
+            return carry
+
+        lax.fori_loop(0, 11, two, 0)
+
     for hop in range(count):
         for part in range(CHUNKS):
             for way in range(2):
@@ -511,7 +557,17 @@
                         slab_copy(owner, way, hop, part, device).start()
 
         if hop == 0:
+            for copy in loads[5:]:
+                copy.wait()
             start_faces(0, 0)
+            absorb(here, True)
+        else:
+            for way in range(2):
+                owner, valid = slab_of(way, hop)
+
+                @pl.when(valid)
+                def _(owner=owner):
+                    absorb(owner, False)
 
     for hop in range(count - 1):
         for part in range(CHUNKS):
@@ -523,22 +579,7 @@
                 def _(owner=owner, way=way, hop=hop, part=part, device=device):
                     slab_copy(owner, way, hop, part, device).wait_send()
 
-    indices = swap_indices()
     low = lane < 64
-
-    def arrange(plane, carry):
-        for tile in range(4):
-            cut = pl.ds(tile * 128, 128)
-            first = jnp.concatenate([gathered[0, plane, :, cut], gathered[1, plane, :, cut]], axis=0)
-            second = jnp.concatenate([gathered[2, plane, :, cut], gathered[3, plane, :, cut]], axis=0)
-            even = jnp.where(low, first, pltpu.roll(second, 64, 1))
-            odd = jnp.where(low, pltpu.roll(first, 64, 1), second)
-            fields[plane, 2 * tile] = swap(even, indices)
-            fields[plane, 2 * tile + 1] = swap(odd, indices)
-        return carry
-
-    lax.fori_loop(0, 22, arrange, 0)
-
     ids = jnp.concatenate([gathered[dev, 22, :, 0:128] for dev in range(4)], axis=0)
     ids = jnp.concatenate([ids, jnp.zeros((112, 128), jnp.float32)], axis=0)
     spread = lax.broadcasted_iota(jnp.int32, (128, 128), 1) // 8
@@ -690,8 +731,8 @@
     upper = here * block_count >= 8
     shift_rows = lax.rem(here * block_count, 8) > 0
 
-    def hand_out(member, carry):
-        scale = jnp.where(member == 0, 3.0, jnp.where(member < 7, 18.0, 36.0))
+    def hand_out_one(member):
+        scale = jnp.where(jnp.asarray(member) == 0, 3.0, jnp.where(jnp.asarray(member) < 7, 18.0, 36.0))
         for tile in range(4):
             even = post[last, member, 2 * tile]
             odd = post[last, member, 2 * tile + 1]
@@ -700,14 +741,23 @@
             rows = swap(jnp.where(upper, upper_part, lower_part), indices) * scale
             rows = jnp.where(shift_rows, pltpu.roll(rows, 4, 0), rows)
             weighted[member, :, pl.ds(tile * 128, 128)] = rows[0:4]
-        return carry
+
+    def hand_out(first, end):
+        def three(at, carry):
+            for more in range(3):
+                hand_out_one(first + 3 * at + more)
+            return carry
+
+        lax.fori_loop(0, (end - first) // 3, three, 0)
+        for member in range(end - (end - first) % 3, end):
+            hand_out_one(member)
 
     for turn in range(TISSUE_STEPS):
         slot = turn % 2
         if turn > 0:
             start_faces(slot, turn)
-            middle = 19 * turn // (TISSUE_STEPS - 1)
-            lax.fori_loop(19 * (turn - 1) // (TISSUE_STEPS - 1), middle, hand_out, 0)
+            first = 19 * (turn - 1) // (TISSUE_STEPS - 1)
+            hand_out(first, 19 * turn // (TISSUE_STEPS - 1))
         wait_faces(slot, turn)
         tissue(slot, turn)
 
@@ -727,9 +777,15 @@
             jax.ShapeDtypeStruct((19, block_count, 512), f32),
             jax.ShapeDtypeStruct(concentrations.shape, f32),
         ),
-        in_specs=[vmem] * 10,
+        in_specs=[pl.BlockSpec(memory_space=pltpu.HBM)] * 10,
         out_specs=(vmem, vmem),
         scratch_shapes=[
+            pltpu.VMEM((block_count, 512), jnp.int32),
+            pltpu.VMEM((block_count, 512), jnp.int32),
+            pltpu.VMEM((block_count, 18), jnp.int32),
+            pltpu.VMEM(owners.shape, jnp.int32),
+            pltpu.VMEM(slots.shape, jnp.int32),
+            pltpu.VMEM(uptake_rate.shape, f32),
             pltpu.VMEM((count, 23, block_count, 512), f32),
             pltpu.VMEM((22, 8, 8, 128), f32),
             pltpu.VMEM((2, 19, 8, 8, 128), f32),
@@ -745,13 +801,14 @@
             pltpu.VMEM((TISSUE_STEPS, 2, 8, 128), f32),
             pltpu.VMEM((TISSUE_STEPS, 2, species + 1, 8, 128), f32),
             pltpu.VMEM((TISSUE_STEPS, 2, 8, 128), f32),
+            pltpu.SemaphoreType.DMA((10,)),
             pltpu.SemaphoreType.DMA((2, count - 1, CHUNKS)),
             pltpu.SemaphoreType.DMA((2, count - 1, CHUNKS)),
             pltpu.SemaphoreType.DMA((TISSUE_STEPS, 6)),
             pltpu.SemaphoreType.DMA((TISSUE_STEPS, 6)),
         ],
         compiler_params=pltpu.CompilerParams(
-            collective_id=0, has_side_effects=True, vmem_limit_bytes=32 * 1024 * 1024
+            collective_id=0, has_side_effects=True, vmem_limit_bytes=64 * 1024 * 1024
         ),
     )(
         populations[:, 0], viscosity[0], links[0], flags[0], neighbours[0], owners, slots,

time: 43.7 us -> 37.2 us (0.85)
  local copies, waits for them, and re-layouts: 7.4 us -> 2.28 us
  Pallas kernels: 35.2 us -> 34.1 us
    unnamed x22 -> x4, local copies, waits for them, and re-layouts: 7.4 us -> 2.28 us
    pallas_call x1, Pallas kernels: 35.2 us -> 34.1 us  [fused(): pl.pallas_call(kernel, out_shape=(jax.ShapeDtypeStruct((19, block_count,...]
where the time goes in v2:
time: 37.2 us; the launch traced here: 37 us
  Pallas kernels  34.1 us (92%)
  local copies, waits for them, and re-layouts  2.28 us (6%)
  between operations  0.65 us (2%)
    pallas_call x1, Pallas kernels, fused(): pl.pallas_call(kernel, out_shape=(jax.ShapeDtypeStruct((19, block_count,...  34.1 us
    unnamed x4, local copies, waits for them, and re-layouts  2.28 us

profile of v2, /device:TPU:0, one launch (start us, length us, event | category | flops | bytes accessed | tf_op | source)
XLA Modules:
  0.0 37.0 jit_solution(12415381418232764959)
XLA Ops:
  0.6 34.1 %shard_map.113 = (f32[19,4,512]{2,1,0:T(4,128)}, f32[4,8,8,128]{3,2,1,0:T(8,128)}) custom-call(f32[19,4,512]{2,1,0:T(4,128)} %bitcast.8, f32[4,512]{1,0:T(4,128)} %bitcast.10, s32[4,512]{1,0:T(4,128)} %bitcast.11, s32[4,512]{1,0:T(4,128)} %bitcast.12, s32[4,18]{1,0:T(4,128)} %bitcast.13, s32[1,16]{1,0:T(1,128)} %owners_in.1, s32[1,16]{1,0:T(1,128)} %slots_in.1, ...), custom_call_target="tpu_custom_call" | custom-call | tf_op jit(solution)/shard_map/pallas_call | solution.py:774
  34.8 0.0 copy-start
  34.8 1.6 %copy.15 = f32[19,1,4,512]{3,2,1,0:T(4,128)} copy(f32[19,1,4,512]{3,2,1,0:T(4,128)} %bitcast.9) | data formatting | bytes 311296
  36.4 0.0 copy-done
  36.4 0.7 %copy.16 = f32[4,8,8,128]{3,2,1,0:T(8,128)} copy(f32[4,8,8,128]{3,2,1,0:T(8,128)S(1)} %copy-done) | data formatting | bytes 262144
Async XLA Ops:
  34.8 1.6 %copy-start = (f32[4,8,8,128]{3,2,1,0:T(8,128)S(1)}, f32[4,8,8,128]{3,2,1,0:T(8,128)}, u32[]{:S(2)}) copy-start(f32[4,8,8,128]{3,2,1,0:T(8,128)} %get-tuple-element.11) | copy-start | bytes 393220

commit v3 on v2

--- a/solution.py
+++ b/solution.py
@@ -375,7 +375,8 @@
 
 def kernel(
     pops, visc, links, flags, beside, owners_in, slots_in, conc, diff, uptake_in,
-    weighted, conc_out,
+    weighted_to, conc_to,
+    weighted, conc_out, store,
     links_at, flags_at, beside_at, owners, slots, uptake, gathered, fields, post, tables, open_bits, relax_by, marks,
     cells, rates, winds, halo_x, halo_y, halo_z, pack_y, pack_z,
     load, send_g, recv_g, send_t, recv_t,
@@ -450,8 +451,9 @@
         )
 
     def start_faces(slot, turn):
-        pack(slot, turn)
         for at, axis in enumerate(AXES):
+            if at == 1:
+                pack(slot, turn)
             for side, (there, device) in enumerate(sides_of(axis)):
 
                 @pl.when(there)
@@ -485,7 +487,7 @@
     gathered[here, 22, :, 0:18] = beside_at[...].astype(jnp.float32)
     pl.semaphore_wait(barrier, expected)
 
-    bounds = [planes * part // CHUNKS for part in range(CHUNKS + 1)]
+    bounds = [0, 12, planes]
     neighbours = sides_of("gx")
 
     def slab_copy(owner, way, hop, part, device):
@@ -512,7 +514,7 @@
         for late in range(2)
     ]
 
-    def absorb(owner, first):
+    def absorb(owner, part, first=False):
         mine = lane // (8 * block_count) == owner
 
         def one(plane):
@@ -536,7 +538,17 @@
             one(2 * at + 1)
             return carry
 
-        lax.fori_loop(0, 11, two, 0)
+        start, end = bounds[part], min(bounds[part + 1], 22)
+        lax.fori_loop(start // 2, end // 2, two, 0)
+
+    toward = jnp.where(here >= count // 2, 1, -1)
+
+    def absorb_at(distance, part):
+        owner = here - distance * toward
+
+        @pl.when(jnp.logical_and(owner >= 0, owner < count))
+        def _():
+            absorb(lax.clamp(0, owner, count - 1), part)
 
     for hop in range(count):
         for part in range(CHUNKS):
@@ -556,18 +568,21 @@
                     def _(owner=owner, way=way, hop=hop, part=part, device=device):
                         slab_copy(owner, way, hop, part, device).start()
 
+            if hop > 0:
+                absorb_at(hop, part)
+
         if hop == 0:
             for copy in loads[5:]:
                 copy.wait()
             start_faces(0, 0)
-            absorb(here, True)
+            for part in range(CHUNKS):
+                absorb(here, part, True)
         else:
-            for way in range(2):
-                owner, valid = slab_of(way, hop)
-
-                @pl.when(valid)
-                def _(owner=owner):
-                    absorb(owner, False)
+            for part in range(CHUNKS):
+                if hop > 1:
+                    absorb_at(1 - hop, part)
+                if hop == count - 1:
+                    absorb_at(-hop, part)
 
     for hop in range(count - 1):
         for part in range(CHUNKS):
@@ -727,6 +742,8 @@
                     conc_out[kind, a] = total
                 else:
                     cells[1 - slot, kind, a] = total
+            if turn == TISSUE_STEPS - 1 and a % 4 == 3:
+                conc_copies[a // 4].start()
 
     upper = here * block_count >= 8
     shift_rows = lax.rem(here * block_count, 8) > 0
@@ -752,14 +769,27 @@
         for member in range(end - (end - first) % 3, end):
             hand_out_one(member)
 
+    weighted_copy = pltpu.make_async_copy(weighted, weighted_to, store.at[2])
+    conc_copies = []
+    for part in range(2):
+        cut = pl.ds(4 * part, 4)
+        conc_copies.append(
+            pltpu.make_async_copy(conc_out.at[:, cut], conc_to.at[:, cut], store.at[part])
+        )
+
     for turn in range(TISSUE_STEPS):
         slot = turn % 2
         if turn > 0:
             start_faces(slot, turn)
             first = 19 * (turn - 1) // (TISSUE_STEPS - 1)
             hand_out(first, 19 * turn // (TISSUE_STEPS - 1))
+        if turn == TISSUE_STEPS - 1:
+            weighted_copy.start()
         wait_faces(slot, turn)
         tissue(slot, turn)
+    for copy in conc_copies:
+        copy.wait()
+    weighted_copy.wait()
 
 
 def fused(
@@ -769,7 +799,7 @@
     count = lax.axis_size("gx")
     block_count = populations.shape[2]
     species = concentrations.shape[0]
-    vmem = pl.BlockSpec(memory_space=pltpu.VMEM)
+    hbm = pl.BlockSpec(memory_space=pltpu.HBM)
     f32 = jnp.float32
     weighted, conc = pl.pallas_call(
         kernel,
@@ -777,9 +807,12 @@
             jax.ShapeDtypeStruct((19, block_count, 512), f32),
             jax.ShapeDtypeStruct(concentrations.shape, f32),
         ),
-        in_specs=[pl.BlockSpec(memory_space=pltpu.HBM)] * 10,
-        out_specs=(vmem, vmem),
+        in_specs=[hbm] * 10,
+        out_specs=(hbm, hbm),
         scratch_shapes=[
+            pltpu.VMEM((19, block_count, 512), f32),
+            pltpu.VMEM(concentrations.shape, f32),
+            pltpu.SemaphoreType.DMA((3,)),
             pltpu.VMEM((block_count, 512), jnp.int32),
             pltpu.VMEM((block_count, 512), jnp.int32),
             pltpu.VMEM((block_count, 18), jnp.int32),

time: 37.2 us -> 35.7 us (0.960)
  Pallas kernels: 34.1 us -> 32.6 us
    pallas_call x1, Pallas kernels: 34.1 us -> 32.6 us  [fused(): pl.pallas_call(kernel, out_shape=(jax.ShapeDtypeStruct((19, block_count,...]
where the time goes in v3:
time: 35.7 us; the launch traced here: 35.6 us
  Pallas kernels  32.6 us (91%)
  local copies, waits for them, and re-layouts  2.28 us (6%)
  between operations  0.65 us (2%)
    pallas_call x1, Pallas kernels, fused(): pl.pallas_call(kernel, out_shape=(jax.ShapeDtypeStruct((19, block_count,...  32.6 us
    unnamed x4, local copies, waits for them, and re-layouts  2.28 us

profile of v3, /device:TPU:0, one launch (start us, length us, event | category | flops | bytes accessed | tf_op | source)
XLA Modules:
  0.0 35.6 jit_solution(16534153138874914744)
XLA Ops:
  0.6 32.6 %shard_map.113 = (f32[19,4,512]{2,1,0:T(4,128)}, f32[4,8,8,128]{3,2,1,0:T(8,128)}) custom-call(f32[19,4,512]{2,1,0:T(4,128)} %bitcast.8, f32[4,512]{1,0:T(4,128)} %bitcast.10, s32[4,512]{1,0:T(4,128)} %bitcast.11, s32[4,512]{1,0:T(4,128)} %bitcast.12, s32[4,18]{1,0:T(4,128)} %bitcast.13, s32[1,16]{1,0:T(1,128)} %owners_in.1, s32[1,16]{1,0:T(1,128)} %slots_in.1, ...), custom_call_target="tpu_custom_call" | custom-call | tf_op jit(solution)/shard_map/pallas_call | solution.py:804
  33.3 0.0 copy-start
  33.3 1.6 %copy.15 = f32[19,1,4,512]{3,2,1,0:T(4,128)} copy(f32[19,1,4,512]{3,2,1,0:T(4,128)} %bitcast.9) | data formatting | bytes 311296
  34.9 0.0 copy-done
  34.9 0.7 %copy.16 = f32[4,8,8,128]{3,2,1,0:T(8,128)} copy(f32[4,8,8,128]{3,2,1,0:T(8,128)S(1)} %copy-done) | data formatting | bytes 262144
Async XLA Ops:
  33.3 1.6 %copy-start = (f32[4,8,8,128]{3,2,1,0:T(8,128)S(1)}, f32[4,8,8,128]{3,2,1,0:T(8,128)}, u32[]{:S(2)}) copy-start(f32[4,8,8,128]{3,2,1,0:T(8,128)} %get-tuple-element.11) | copy-start | bytes 393220
